TPU v7x, 128 devices: a whole 4x4x4 slice. The times are simulated.
128 devices in a mesh: ta: 8 (over y, core), xyz: 16 (over x, z).
Axes of the slice: x: 4, y: 4, z: 4, core: 2. Of those that a mesh axis runs over, the one named last changes fastest.
Arguments:
- source: float32 [4, 2, 32, 128, 4, 128], P(None, None, 'ta', 'xyz'), may hold values from -6 to 6
- mass: float32 [32, 128, 4, 128], P('ta', 'xyz'), may hold values from 0.2 to 4
- links: int32 [4, 32, 128, 4, 128], P(None, 'ta', 'xyz'), may hold values from 0 to 1
- near_null: bfloat16 [24, 4, 32, 128, 4, 128], P(None, None, 'ta', 'xyz'), may hold values from -0.1875 to 0.1875
- coarse_op: bfloat16 [9, 24, 24, 8, 32, 1, 32], P(None, None, None, 'ta', 'xyz'), may hold values from -0.09 to 1.1
- plan: int32 [8], replicated, may hold values from 0 to 1
Outputs:
- solution: float32 [4, 2, 32, 128, 4, 128], P(None, None, 'ta', 'xyz')
- residual: float32 [4, 2, 32, 128, 4, 128], P(None, None, 'ta', 'xyz')
All inputs are finite; a program needn't handle non-finite values.
Results may differ from a plain program's by a relative error of at most 0.011.
Values may be sent and summed in bfloat16 or wider, within the bound.
No kernel may reach another device: no remote copies, remote signals or barrier semaphores. Data moves between devices by JAX's collectives and lax.ppermute only.
A program may use at most 192 MiB of HBM per device.

v0:
```python
import functools

import jax
import jax.numpy as jnp
from jax import lax
from jax.experimental import pallas as pl
from jax.experimental.pallas import tpu as pltpu
from jax.sharding import PartitionSpec as P

LT, ROWS, LANES = 4, 32, 128
NVEC, RHS, KC, SWEEPS = 24, 2, 6, 8
ET, EROWS, PAD = 14, 80, 8
T0, OWN = 5, (24, ROWS)
FIELDS = 13
F32, BF16, I32 = jnp.float32, jnp.bfloat16, jnp.int32


def params(mebibytes):
    return pltpu.CompilerParams(vmem_limit_bytes=int(mebibytes * 1024 * 1024))


def shape(dims, dtype):
    return jax.ShapeDtypeStruct(dims, dtype)


VM = pl.BlockSpec(memory_space=pltpu.VMEM)
HB = pl.BlockSpec(memory_space=pltpu.HBM)


def roll(values, shift, axis):
    return pltpu.roll(values, shift, axis)


def tile_iotas():
    row = lax.broadcasted_iota(I32, (8, LANES), 0)
    lane = lax.broadcasted_iota(I32, (8, LANES), 1)
    return row, lane


def turns(v):
    along_y = (roll(v[0], 2, 0), roll(v[1], 6, 0), roll(v[2], 6, 0), roll(v[3], 2, 0))
    f, g = roll(v[0] + v[3], LANES - 1, 1), roll(v[1] - v[2], LANES - 1, 1)
    h, k = roll(v[0] - v[3], 1, 1), roll(v[1] + v[2], 1, 1)
    return along_y, (f, g, h, k)


def hops(turned, before, after, ahead_t, behind_t, coefs):
    sign_t, sign_x, sign_y, sign_z = coefs
    p0, p1 = ahead_t[0] - ahead_t[2], ahead_t[1] - ahead_t[3]
    q0, q1 = behind_t[0] + behind_t[2], behind_t[1] + behind_t[3]
    along_t = (q0 + p0, q1 + p1, q0 - p0, q1 - p1)
    u0, u2 = after[0] - after[1], after[2] + after[3]
    w0, w2 = before[0] + before[1], before[2] - before[3]
    along_x = (w0 + u0, w0 - u0, u2 + w2, u2 - w2)
    along_y, (f, g, h, k) = turned
    along_z = (f + h, k + g, k - g, f - h)
    return [
        (sign_t * along_t[s] + sign_x * along_x[s]) + (sign_y * along_y[s] + sign_z * along_z[s])
        for s in range(4)
    ]


def layer_rows(layer):
    start = 2 * PAD + 8 * layer
    return slice(start, start + 8)


def visit(field, signs, slices, tiles, put):
    lows = slices[0::2]
    length = slices[1] - slices[0]

    def spins_at(time, layer):
        return [field[s, time, layer_rows(layer), :] for s in range(4)]

    def layers_of(t, first, last):
        spins, turned = {first - 1: spins_at(t, first - 1)}, {}

        def prepare(layer):
            if layer <= last:
                spins[layer] = spins_at(t, layer)
            if layer < last:
                turned[layer] = turns(spins[layer])

        for layer in range(first, first + 2):
            prepare(layer)
        for layer in range(first, last):
            prepare(layer + 2)
            coefs = [signs[m, t, layer_rows(layer), :] for m in range(4)]
            sums = hops(
                turned[layer], spins[layer - 1], spins[layer + 1], spins_at(t + 1, layer), spins_at(t - 1, layer), coefs
            )
            put(t, layer, spins[layer], sums)

    def body(step, carry):
        t = step + lows[0] if len(lows) == 1 else jnp.where(step < length, step + lows[0], step - length + lows[1])
        for low, high in zip(tiles[0::2], tiles[1::2]):
            layers_of(t, 2 * low, 2 * high)
        return carry

    lax.fori_loop(0, length * len(lows), body, 0, unroll=min(4, length * len(lows)))


def chosen(plan, colour, t, layer, lane):
    block = lax.axis_index("ta") + (t + 3) // 4 + layer // 4 + 1
    return ((lane >> 2) & 1) == ((plan[colour] + block) & 1)


def half_sweep(plan, colour, target, field, source, signs, inverse, slices, tiles, lane):
    def put(t, layer, centre, sums):
        rows = layer_rows(layer)
        mask = chosen(plan, colour, t, layer, lane)
        scale = inverse[t, rows, :]
        for s in range(4):
            value = (source[s, t, rows, :] + sums[s]) * scale
            target[s, t, rows, :] = jnp.where(mask, value, centre[s])

    visit(field, signs, slices, tiles, put)


EARLY = (((6, 8), (0, 8)), ((5, 6, 8, 9), (2, 6)), ((2, 5, 9, 12), (3, 5)))
LATE = {
    3: (((5, 6, 8, 9), (0, 2, 6, 8)), ((3, 5, 9, 11), (1, 3, 5, 7)), ((2, 3, 11, 12), (2, 3, 5, 6))),
    4: (
        ((5, 6, 8, 9), (0, 2, 6, 8)),
        ((4, 5, 9, 10), (0, 3, 5, 8)),
        ((2, 4, 10, 12), (1, 3, 5, 7)),
        ((1, 2, 12, 13), (2, 6)),
    ),
}


def part_sweep(plan, colour, parts, target, field, src, signs, inverse, lane):
    for slices, tiles in parts:
        half_sweep(plan, colour, target, field, src, signs, inverse, slices, tiles, lane)


def first_values(plan, target, src, inverse, lane, low, high, layers):
    def one_slice(t, carry):
        for layer in layers:
            rows = layer_rows(layer)
            scale = jnp.where(chosen(plan, 0, t, layer, lane), inverse[t, rows, :], 0.0)
            for s in range(4):
                target[s, t, rows, :] = src[s, t, rows, :] * scale
        return carry

    lax.fori_loop(low, high, one_slice, 0)


OWN_LAYERS, HALO_LAYERS = tuple(range(4, 12)), (0, 1, 2, 3, 12, 13, 14, 15)


def wide_sweep(plan, colour, depth, target, field, src, signs, inverse, lane):
    done = 0
    while done <= depth:
        tiles = (2, 6) if depth == done else (1, 7) if depth - done <= 2 else (0, 8)
        last = depth if depth == done else depth - 1 if depth - done <= 2 else depth - 3
        if done == 0:
            slices = (T0 - last, T0 + LT + last)
        else:
            slices = (T0 - last, T0 - done + 1, T0 + LT + done - 1, T0 + LT + last)
        half_sweep(plan, colour, target, field, src, signs, inverse, slices, tiles, lane)
        done = last + 1


def places():
    t_odd, x_odd = lax.axis_index("ta") & 1, lax.axis_index("xyz") & 1
    return (t_odd, 1 - t_odd), (x_odd, 1 - x_odd)


def x_start(before):
    return PAD + 48 * (1 - before)


def side_rows(rows, n):
    return pl.ds(2 * rows[0] + n, rows[1], stride=2)


def column_of(data, t, before, first):
    pair = data[8 * (t // 2) : 8 * (t // 2) + 8]
    turned = roll(pair, 4, 0)
    top, bottom = (pair, turned) if t % 2 == 0 else (turned, pair)
    return jnp.where(before == 0, jnp.where(first, top, 0.0), jnp.where(first, 0.0, bottom))


def put_cross(fields, ta, tb, xa, xb, put, add_low, first):
    t_before, x_before = places()
    for data, before in ((ta, t_before[0]), (tb, t_before[1])):
        for part in range(2):
            base = T0 + LT - 8 * before + 2 * part

            def t_slice(t, carry, data=data[part], base=base):
                for c in range(fields):
                    put(c, base + t, OWN, data[fields * t + c].astype(F32))
                return carry

            lax.fori_loop(0, 2, t_slice, 0)
        near = T0 + LT - 5 * before
        for c in range(8):
            add_low(c, near, OWN, data[c // 4][2 * fields + c % 4].astype(F32))
    for data, before in ((xa, x_before[0]), (xb, x_before[1])):
        start = x_start(before)

        def x_slice(t, carry, data=data, start=start):
            for c in range(fields):
                put(c, T0 + t, (start, 16), data[fields * t + c].astype(F32))
            return carry

        lax.fori_loop(0, LT, x_slice, 0)
        where = (start + 8 * before, 8)
        for c in range(8):
            low = data[4 * fields + c].astype(F32)
            for t in range(LT):
                add_low(c, T0 + t, where, column_of(low, t, before, first))


def put_corners(fields, ca, cb, put, deep):
    t_before, x_before = places()
    for data, before in ((ca, t_before[0]), (cb, t_before[1])):
        near, step = T0 + LT - 5 * before, 1 - 2 * before
        for half in range(2):
            start = x_start(x_before[half])
            facing = (start + 8 * x_before[half], 8)
            part = slice(16 * half, 16 * half + 16)
            for c in range(fields):
                put(c, near, (start, 16), data[c, part, :].astype(F32))
                if deep:
                    put(c, near + step, (start, 16), data[fields + c, part, :].astype(F32))
                value = data[(1 + deep) * fields + c, part, :].astype(F32)
                put(c, near + (1 + deep) * step, facing, value[:8])
                put(c, near + (2 + deep) * step, facing, value[8:])
        if deep:
            for c in range(fields):
                put(c, (ET - 1) * (1 - before), OWN, data[3 * fields + c].astype(F32))


def low_part(value):
    return value - value.astype(BF16).astype(F32)


def pack_t(fields, read, t_a, t_b):
    t_before, _ = places()
    for part in range(2):

        def one_slice(t, carry, part=part):
            for c in range(fields):
                value = read(c, 2 * part + t).astype(BF16)
                t_a[part][fields * t + c] = value
                t_b[part][fields * t + c] = value
            return carry

        lax.fori_loop(0, 2, one_slice, 0)
    for c in range(8):
        for out, before in ((t_a, t_before[0]), (t_b, t_before[1])):
            out[c // 4][2 * fields + c % 4] = low_part(read(c, 3 * (1 - before))).astype(BF16)


def pack_x(fields, read, x_a, x_b, first):
    _, x_before = places()

    def one_slice(t, carry):
        for c in range(fields):
            value = read(c, t).astype(BF16)
            x_a[fields * t + c] = jnp.where(x_before[0] == 0, value[16:], value[:16])
            x_b[fields * t + c] = jnp.where(x_before[1] == 0, value[16:], value[:16])
        return carry

    lax.fori_loop(0, LT, one_slice, 0)

    def join(tops, bottoms):
        return jnp.concatenate([jnp.where(first, tops[t], bottoms[t + 1]) for t in (0, 2)], 0)

    def turn(values):
        return [roll(value, 4, 0) for value in values]

    for c in range(8):
        values = [read(c, t) for t in range(LT)]
        lows = [low_part(value[:8]) for value in values]
        highs = [low_part(value[24:]) for value in values]
        low, high = join(lows, turn(lows)), join(turn(highs), highs)
        for out, before in ((x_a, x_before[0]), (x_b, x_before[1])):
            out[4 * fields + c] = jnp.where(before == 0, high, low).astype(BF16)
        if x_a.shape[0] > 4 * fields + 8:
            lows = [value[16:24] for value in values]
            highs = [value[8:16] for value in values]
            low, high = join(lows, turn(lows)), join(turn(highs), highs)
            for out, before in ((x_a, x_before[0]), (x_b, x_before[1])):
                out[4 * fields + 8 + c] = jnp.where(before == 0, high, low).astype(BF16)


def corner_kernel(fields, deep, *refs):
    xb, xa, *beyond, ca, cb = refs
    t_before, x_before = places()
    for out, before, behind in ((ca, t_before[0], beyond[2:]), (cb, t_before[1], beyond[:2])):
        if deep:
            for c in range(fields):
                out[3 * fields + c] = jnp.where(before == 1, behind[0][c], behind[1][fields + c])
        near, step = 3 * (1 - before), 2 * before - 1

        def one_field(c, carry, out=out, near=near, step=step):
            for half, data in enumerate((xa, xb)):
                where = slice(16 * half, 16 * half + 16)
                for depth in range(1 + deep):
                    out[depth * fields + c, where, :] = data[fields * (near + depth * step) + c]
                pieces = []
                for depth in (1 + deep, 2 + deep):
                    value = data[fields * (near + depth * step) + c].astype(F32)
                    pieces.append(jnp.where(x_before[half] == 0, value[:8], value[8:]))
                out[(1 + deep) * fields + c, where, :] = jnp.concatenate(pieces, 0).astype(BF16)
            return carry

        lax.fori_loop(0, fields, one_field, 0)


def input_reader(source, mass, links):
    def read(c, t):
        if c < 8:
            return source[c, t]
        if c == 8:
            return mass[t]
        return (1.0 if c == 11 else 0.5) * (1 - 2 * links[c - 9, t]).astype(F32)

    return read


def field_writer(field):
    def put(c, t, rows, value):
        field[c // 2, t, side_rows(rows, c % 2), :] = value

    return put


def input_writer(src, signs, inverse):
    put_source = field_writer(src)

    def put(c, t, rows, value):
        if c < 8:
            put_source(c, t, rows, value)
            return
        if c == 8:
            value = 1.0 / (4.0 + value)
        for n in range(RHS):
            if c == 8:
                inverse[t, side_rows(rows, n), :] = value
            else:
                signs[c - 9, t, side_rows(rows, n), :] = value

    return put


def adder(field):
    def add_low(c, t, rows, value):
        where = side_rows(rows, c % 2)
        field[c // 2, t, where, :] = field[c // 2, t, where, :] + value

    return add_low


def load_kernel(source, mass, links, source_out, mass_out, links_out, x_a, x_b, sems):
    pairs = ((source, source_out), (mass, mass_out), (links, links_out))
    copies = [pltpu.make_async_copy(a, b, sems.at[i]) for i, (a, b) in enumerate(pairs)]
    for copy in copies:
        copy.start()
    for copy in copies:
        copy.wait()
    first = lax.broadcasted_iota(I32, (8, LANES), 0) < 4
    pack_x(FIELDS, input_reader(source_out, mass_out, links_out), x_a, x_b, first)


def share_kernel(source, mass, links, *shares):
    pack_t(FIELDS, input_reader(source, mass, links), shares[:2], shares[2:])


def cross_kernel(
    xb, xa, tb2, tb1, ta2, ta1, source, mass, links, coarse_far, plan_far,
    src, signs, inverse, field_a, field_b, operator,
    coarse, plan, sems,
):
    plan_copy = pltpu.make_async_copy(plan_far, plan, sems.at[0])
    plan_copy.start()
    copy = pltpu.make_async_copy(coarse_far, coarse, sems.at[1])
    copy.start()
    read, put = input_reader(source, mass, links), input_writer(src, signs, inverse)

    def own_slice(t, carry):
        for c in range(FIELDS):
            put(c, t + T0, OWN, read(c, t))
        return carry

    lax.fori_loop(0, LT, own_slice, 0)
    first = lax.broadcasted_iota(I32, (8, LANES), 0) < 4
    put_cross(FIELDS, (ta1, ta2), (tb1, tb2), xa, xb, put, adder(src), first)
    plan_copy.wait()
    _, lane = tile_iotas()
    first_values(plan, field_a, src, inverse, lane, 1, ET - 1, OWN_LAYERS)
    first_values(plan, field_a, src, inverse, lane, T0, T0 + LT, HALO_LAYERS)
    part_sweep(plan, 1, EARLY, field_b, field_a, src, signs, inverse, lane)
    copy.wait()
    relayout(coarse, operator)


def relayout(operator, result):
    def group(kk, carry):
        def block(b, q):
            return operator[b, 4 * kk + q].astype(F32)

        for place, kinds in enumerate(((0, 5, 6), (1,), (2,), (3,), (4,), (7,), (8,))):
            pieces = []
            for q in range(4):
                piece = block(kinds[0], q)
                for b in kinds[1:]:
                    piece = piece + block(b, q)
                pieces.append(piece)
            result[place, kk] = jnp.concatenate(pieces, axis=-1)
        return carry

    lax.fori_loop(0, 6, group, 0)


def exact_sum(matrix, values, left):
    high = values.astype(BF16)
    low = (values - high.astype(F32)).astype(BF16)

    def one(part):
        pair = (matrix, part) if left else (part, matrix)
        return jnp.dot(*pair, preferred_element_type=F32)

    return one(high) + one(low)


def fill_diag(mass, diag):
    for t in range(LT):
        for n in range(RHS):
            diag[t, side_rows((0, ROWS), n), :] = 4.0 + mass[t]


def copy_own(field, first_slice, rows, out):
    def one_slice(t, carry):
        for c in range(8):
            out[c, t] = field[c // 2, t + first_slice, side_rows(rows, c % 2), :]
        return carry

    lax.fori_loop(0, LT, one_slice, 0)


def pre_kernel(
    plan_far, mass, ca, cb, src_in, signs_in, inverse_in, field_a_in, field_b_in, near_null,
    out_solution, out_rhs, out_rounded, src, signs, inverse, field_a, field_b,
    diag, resid, sums, plan, sem,
):
    del src_in, signs_in, inverse_in, field_a_in, field_b_in
    plan_copy = pltpu.make_async_copy(plan_far, plan, sem)
    plan_copy.start()
    _, lane = tile_iotas()
    put_corners(FIELDS, ca, cb, input_writer(src, signs, inverse), 0)
    plan_copy.wait()

    first_values(plan, field_a, src, inverse, lane, 1, T0, HALO_LAYERS)
    first_values(plan, field_a, src, inverse, lane, T0 + LT, ET - 1, HALO_LAYERS)
    common = (src, signs, inverse, lane)
    part_sweep(plan, 1, LATE[3], field_b, field_a, *common)
    wide_sweep(plan, 2, 2, field_a, field_b, *common)
    wide_sweep(plan, 3, 1, field_b, field_a, *common)

    fill_diag(mass, diag)

    def put(t, layer, centre, hop):
        rows, inner = layer_rows(layer), slice(8 * layer - 32, 8 * layer - 24)
        for s in range(4):
            value = (src[s, t, rows, :] - diag[t - T0, inner, :] * centre[s]) + hop[s]
            resid[s, t - T0, inner, :] = value.astype(BF16).astype(F32)

    visit(field_b, signs, (T0, T0 + LT), (2, 6), put)
    copy_own(field_b, T0, OWN, out_solution)
    group = 4

    def vectors(step, carry):
        totals = {}
        for s in range(4):
            for t in range(LT):
                for block in range(2):
                    low, mid, high = 16 * block, 16 * block + 8, 16 * block + 16
                    halves = [
                        (resid[s, t, side_rows((low, 8), n), :], resid[s, t, side_rows((mid, 8), n), :]) for n in range(RHS)
                    ]
                    for i in range(group):
                        vector = near_null[group * step + i, s, t, low:high, :].astype(F32)
                        for n in range(RHS):
                            term = vector[:8] * halves[n][0] + vector[8:] * halves[n][1]
                            key = (i, n, block)
                            totals[key] = term if key not in totals else totals[key] + term
        for (i, n, block), value in totals.items():
            place = 8 * (48 * n + 2 * (group * step + i) + block)
            sums[pl.ds(pl.multiple_of(place, 8), 8), :] = value
        return carry

    lax.fori_loop(0, NVEC // group, vectors, 0)
    count = 2 * NVEC * RHS
    fold = jnp.where(
        lax.broadcasted_iota(I32, (count, 8 * count), 1) >> 3 == lax.broadcasted_iota(I32, (count, 8 * count), 0), 1.0, 0.0
    ).astype(BF16)
    spread = jnp.where(
        lax.broadcasted_iota(I32, (LANES, LANES), 0) >> 2 == lax.broadcasted_iota(I32, (LANES, LANES), 1) & 31, 1.0, 0.0
    ).astype(BF16)
    rhs = exact_sum(spread, exact_sum(fold, sums[...], True), False)
    out_rhs[...] = rhs
    out_rounded[...] = rhs.astype(BF16)


def coarse_step(operator, rhs, estimate, rounded, ta, tb, xa, xb, beside, out):
    row, lane = tile_iotas()
    t_odd, x_odd = lax.axis_index("ta") & 1, lax.axis_index("xyz") & 1
    even_row = (row & 1) == 0
    for i in range(12):
        where = slice(8 * i, 8 * i + 8)
        own = rounded[where].astype(F32)
        t_first, t_second = ta[where].astype(F32), tb[where].astype(F32)
        x_first, x_second = xa[where].astype(F32), xb[where].astype(F32)
        beside[0, where] = own
        beside[1, where] = jnp.where(t_odd == 0, t_first, t_second)
        beside[2, where] = jnp.where(t_odd == 0, t_second, t_first)
        after = jnp.where(x_odd == 0, x_first, x_second)
        before = jnp.where(x_odd == 0, x_second, x_first)
        own_up, own_down = roll(own, 7, 0), roll(own, 1, 0)
        beside[3, where] = jnp.where(even_row, own_up, roll(after, 1, 0))
        beside[4, where] = jnp.where(even_row, roll(before, 7, 0), own_down)
        beside[5, where] = roll(own, LANES - 1, 1)
        beside[6, where] = roll(own, 1, 1)
    totals = [[None] * RHS for _ in range(6)]
    for b in range(7):
        near = [[beside[b, 48 * n + 8 * j : 48 * n + 8 * j + 8, :] for j in range(6)] for n in range(RHS)]
        for kk in range(6):
            for j in range(6):
                block = operator[b, kk, 8 * j : 8 * j + 8, :]
                for n in range(RHS):
                    term = block * near[n][j]
                    totals[kk][n] = term if totals[kk][n] is None else totals[kk][n] + term
    diagonal = (lane >> 5) == (row >> 1)
    for n in range(RHS):
        for kk in range(6):
            where = slice(48 * n + 8 * kk, 48 * n + 8 * kk + 8)
            value = totals[kk][n]
            value = value + roll(value, 4, 0)
            value = value + roll(value, 2, 0)
            value = jnp.where(diagonal, value, 0.0)
            value = value + roll(value, 64, 1)
            value = value + roll(value, 32, 1)
            out[where] = estimate[where] + (rhs[where] - value)


def coarse_kernel(operator, rhs, estimate, rounded, ta, tb, xa, xb, out, out_rounded, beside):
    coarse_step(operator, rhs, estimate, rounded, ta, tb, xa, xb, beside, out)
    out_rounded[...] = out[...].astype(BF16)


def prolong_kernel(
    operator, rhs, estimate, rounded, ta, tb, xa, xb, near_null, solution,
    out, x_a, x_b,
    beside, final, spread_rows,
):
    coarse_step(operator, rhs, estimate, rounded, ta, tb, xa, xb, beside, final)
    widen = jnp.where(
        lax.broadcasted_iota(I32, (LANES, LANES), 0) == lax.broadcasted_iota(I32, (LANES, LANES), 1) >> 2, 1.0, 0.0
    ).astype(BF16)
    wide = jnp.dot(final[...].astype(BF16), widen, preferred_element_type=F32)
    for i in range(2 * NVEC * RHS):
        spread_rows[i] = jnp.broadcast_to(wide[i : i + 1, :], (8, LANES))

    def body(step, carry):
        pair, t = step // LT, step % LT
        spins = (2 * pair, 2 * pair + 1)
        for block in range(2):
            low, mid, high = 16 * block, 16 * block + 8, 16 * block + 16
            totals = {}
            for k in range(NVEC):
                weights = [spread_rows[48 * n + 2 * k + block] for n in range(RHS)]
                for i, s in enumerate(spins):
                    vector = near_null[k, s, t, low:high, :].astype(F32)
                    for n in range(RHS):
                        for part in range(2):
                            term = vector[8 * part : 8 * part + 8] * weights[n]
                            key = (i, n, part)
                            totals[key] = term if k == 0 else totals[key] + term
            for i, s in enumerate(spins):
                for n in range(RHS):
                    for part, span in enumerate((slice(low, mid), slice(mid, high))):
                        out[2 * s + n, t, span, :] = solution[2 * s + n, t, span, :] + totals[i, n, part]
        return carry

    lax.fori_loop(0, 2 * LT, body, 0)
    first = lax.broadcasted_iota(I32, (8, LANES), 0) < 4
    pack_x(8, lambda c, t: out[c, t], x_a, x_b, first)


def share_field_kernel(solution, *shares):
    pack_t(8, lambda c, t: solution[c, t], shares[:2], shares[2:])


def field_kernel(
    xb, xa, tb2, tb1, ta2, ta1, solution, src, signs, inverse, plan_far, field, swept, plan, sem
):
    plan_copy = pltpu.make_async_copy(plan_far, plan, sem)
    plan_copy.start()
    put = field_writer(field)

    def own_slice(t, carry):
        for c in range(8):
            put(c, t + T0, OWN, solution[c, t])
        return carry

    lax.fori_loop(0, LT, own_slice, 0)
    first = lax.broadcasted_iota(I32, (8, LANES), 0) < 4
    put_cross(8, (ta1, ta2), (tb1, tb2), xa, xb, put, adder(field), first)
    _, x_before = places()
    for data, before in ((xa, x_before[0]), (xb, x_before[1])):
        where = ((EROWS - 8) * (1 - before), 8)
        for c in range(8):
            layer = data[40 + c].astype(F32)
            for t in range(LT):
                put(c, T0 + t, where, column_of(layer, t, before, first))
    plan_copy.wait()
    _, lane = tile_iotas()
    part_sweep(plan, 4, EARLY, swept, field, src, signs, inverse, lane)


def post_kernel(
    plan_far, mass, src, signs, inverse, field_a_in, field_b_in, ca, cb,
    out, residual, field_a, field_b,
    diag, resid, plan, sem,
):
    del field_a_in, field_b_in
    plan_copy = pltpu.make_async_copy(plan_far, plan, sem)
    plan_copy.start()
    row, lane = tile_iotas()

    put_corners(8, ca, cb, field_writer(field_a), 1)
    fill_diag(mass, diag)
    plan_copy.wait()
    common = (src, signs, inverse, lane)
    part_sweep(plan, 4, LATE[4], field_b, field_a, *common)
    wide_sweep(plan, 5, 3, field_a, field_b, *common)
    wide_sweep(plan, 6, 2, field_b, field_a, *common)
    wide_sweep(plan, 7, 1, field_a, field_b, *common)

    def put(t, layer, centre, hop):
        rows, inner = layer_rows(layer), slice(8 * layer - 32, 8 * layer - 24)
        for s in range(4):
            resid[s, t - T0, inner, :] = (src[s, t, rows, :] - diag[t - T0, inner, :] * centre[s]) + hop[s]

    visit(field_a, signs, (T0, T0 + LT), (2, 6), put)
    copy_own(field_a, T0, OWN, out)
    copy_own(resid, 0, (0, ROWS), residual)


def call(kernel, mebibytes, outs, scratch, *args, aliases=(), far=(), cost=None):
    scratch = [item if not isinstance(item, tuple) else pltpu.VMEM(item, F32) for item in scratch]
    specs = [HB if i in far else VM for i in range(len(args))]
    return pl.pallas_call(
        kernel,
        out_shape=outs,
        in_specs=specs,
        out_specs=[VM] * len(outs),
        scratch_shapes=scratch,
        input_output_aliases=dict(aliases),
        compiler_params=params(mebibytes),
        cost_estimate=cost and pl.CostEstimate(flops=cost, bytes_accessed=cost, transcendentals=0),
    )(*args)


def swap(values, axis, odd_pairs):
    devices = lax.axis_size(axis)
    if odd_pairs:
        pairs = [(i, (i + 1) % devices if i % 2 else (i - 1) % devices) for i in range(devices)]
    else:
        pairs = [(i, i ^ 1) for i in range(devices)]
    return lax.ppermute(values, axis, pairs)


def swap_four(t_first, t_second, x_first, x_second):
    xb = swap(x_second, "xyz", True)
    xa = swap(x_first, "xyz", False)
    tb = swap(t_second, "ta", True)
    ta = swap(t_first, "ta", False)
    return ta, tb, xa, xb


def slabs(count, rows):
    return shape((count, rows, LANES), BF16)


def swap_six(ta1, ta2, tb1, tb2, x_first, x_second):
    xb = swap(x_second, "xyz", True)
    xa = swap(x_first, "xyz", False)
    second = [swap(part, "ta", True) for part in (tb1, tb2)]
    return *(swap(part, "ta", False) for part in (ta1, ta2)), *second, xa, xb


def corners_of(fields, deep, *near):
    kernel = functools.partial(corner_kernel, fields, deep)
    *t_parts, xa, xb = near
    beyond = t_parts if deep else ()
    ca, cb = call(kernel, 4, [slabs((2 + 2 * deep) * fields, ROWS)] * 2, [], xb, xa, *beyond)
    cb = swap(cb, "ta", True)
    return swap(ca, "ta", False), cb


def per_device(source, mass, links, near_null, coarse_op, plan):
    out_shape = source.shape
    source = source.reshape(8, LT, ROWS, LANES)
    mass = mass.reshape(LT, ROWS, LANES)
    links = links.reshape(4, LT, ROWS, LANES)
    near_null = near_null.reshape(NVEC, 4, LT, ROWS, LANES)
    coarse_op = coarse_op.reshape(9, NVEC, 2 * NVEC, 32)
    count = 2 * NVEC * RHS
    field, own, ext = (8, LT, ROWS, LANES), (4, LT, 2 * ROWS, LANES), (4, ET, 2 * EROWS, LANES)
    inputs = [shape(ext, F32), shape(ext, F32), shape(ext[1:], F32)]

    plan = pltpu.with_memory_space_constraint(plan, pltpu.HBM)
    source, mass, links, x_a, x_b = call(
        load_kernel,
        8,
        [shape(field, F32), shape(field[1:], F32), shape((4, *field[1:]), I32)] + [slabs(4 * FIELDS + 8, 16)] * 2,
        [pltpu.SemaphoreType.DMA((3,))],
        *(pltpu.with_memory_space_constraint(value, pltpu.HBM) for value in (source, mass, links)),
        far=(0, 1, 2),
    )
    shares = call(share_kernel, 6, [slabs(2 * FIELDS + 4, ROWS)] * 4, [], source, mass, links, cost=1 << 22)
    near = swap_six(*shares, x_a, x_b)
    corners = corners_of(FIELDS, 0, *near)
    coarse_op = pltpu.with_memory_space_constraint(coarse_op, pltpu.HBM)
    *inputs_near, operator = call(
        cross_kernel,
        10,
        inputs + [shape(ext, F32)] * 2 + [shape((7, 6, 2 * NVEC, LANES), F32)],
        [pltpu.VMEM(coarse_op.shape, BF16), pltpu.SMEM((SWEEPS,), I32), pltpu.SemaphoreType.DMA((2,))],
        *near[::-1], source, mass, links, coarse_op, plan,
        far=(9, 10),
        cost=1 << 22,
    )
    solution, rhs, rounded, src, signs, inverse, *_ = call(
        pre_kernel,
        12,
        [shape(field, F32), shape((count, LANES), F32), shape((count, LANES), BF16)] + inputs + [shape(ext, F32)] * 2,
        [(LT, 2 * ROWS, LANES), own, (8 * count, LANES), pltpu.SMEM((SWEEPS,), I32), pltpu.SemaphoreType.DMA],
        plan, mass, *corners, *inputs_near, near_null,
        aliases=((4, 3), (5, 4), (6, 5), (7, 6), (8, 7)),
        far=(0,),
    )
    estimate = rhs
    beside = (7, count, LANES)
    for turn in range(1, KC):
        near = swap_four(rounded, rounded, rounded, rounded)
        given = (operator, rhs, estimate, rounded, *near)
        if turn < KC - 1:
            outs = [shape((count, LANES), F32), shape((count, LANES), BF16)]
            estimate, rounded = call(coarse_kernel, 6, outs, [beside], *given)
    solution, x_a, x_b = call(
        prolong_kernel,
        12,
        [shape(field, F32)] + [slabs(48, 16)] * 2,
        [beside, (count, LANES), (count, 8, LANES)],
        *given, near_null, solution,
    )
    shares = call(share_field_kernel, 4, [slabs(20, ROWS)] * 4, [], solution, cost=1 << 22)
    near = swap_six(*shares, x_a, x_b)
    corners = corners_of(8, 1, *near)
    plan_scratch = [pltpu.SMEM((SWEEPS,), I32), pltpu.SemaphoreType.DMA]
    grown = call(
        field_kernel,
        8,
        [shape(ext, F32)] * 2,
        plan_scratch,
        *near[::-1], solution, src, signs, inverse, plan,
        far=(10,),
        cost=1 << 22,
    )
    solution, residual, *_ = call(
        post_kernel,
        12,
        [shape(field, F32)] * 2 + [shape(ext, F32)] * 2,
        [(LT, 2 * ROWS, LANES), own] + plan_scratch,
        plan, mass, src, signs, inverse, *grown, *corners,
        aliases=((5, 2), (6, 3)),
        far=(0,),
    )
    return solution.reshape(out_shape), residual.reshape(out_shape)


def solution(mesh):
    return jax.shard_map(
        per_device,
        mesh=mesh,
        in_specs=(
            P(None, None, "ta", "xyz", None, None),
            P("ta", "xyz", None, None),
            P(None, "ta", "xyz", None, None),
            P(None, None, "ta", "xyz", None, None),
            P(None, None, None, "ta", "xyz", None, None),
            P(),
        ),
        out_specs=(P(None, None, "ta", "xyz", None, None), P(None, None, "ta", "xyz", None, None)),
        check_vma=False,
    )
```

profile of v0, /device:TPU:0, one launch (start us, length us, event | category | flops | bytes accessed | tf_op | source)
XLA Modules:
  0.0 92.4 jit_solution(885966129296373072)
XLA Ops:
  0.6 1.5 %shard_map.77 = (f32[8,4,32,128]{3,2,1,0:T(8,128)S(1)}, f32[4,32,128]{2,1,0:T(8,128)S(1)}, s32[4,4,32,128]{3,2,1,0:T(8,128)S(1)}, bf16[60,16,128]{2,1,0:T(8,128)(2,1)S(1)}, bf16[60,16,128]{2,1,0:T(8,128)(2,1)S(1)}) custom-call(f32[8,4,32,128]{3,2,1,0:T(8,128)} %bitcast.10, f32[4,32,128]{2,1,0:T(8,128)} %bitcast.12, s32[4,4,32,128]{3,2,1,0:T(8,128)} %bitcast.11), custom_call_target="tpu_custom_call" | custom-call | tf_op jit(solution)/shard_map/pallas_call | solution.py:657
  2.1 6.4 %collective-permute-start = (bf16[60,16,128]{2,1,0:T(8,128)(2,1)S(1)}, bf16[60,16,128]{2,1,0:T(8,128)(2,1)S(1)}, u32[]{:S(2)}, u32[]{:S(2)}) collective-permute-start(bf16[60,16,128]{2,1,0:T(8,128)(2,1)S(1)} %get-tuple-element.47), channel_id=1, source_target_pairs={{0,15},{1,2},{2,1},{3,4},{4,3},{5,6},{6,5},{7,8},{8,7},{9,10},{10,... | collective-permute-start | bytes 737288 | tf_op jit(solution)/shard_map/ppermute | solution.py:675
  8.5 0.1 shard_map.79
  8.6 2.3 %collective-permute-start.4 = (bf16[30,32,128]{2,1,0:T(8,128)(2,1)S(1)}, bf16[30,32,128]{2,1,0:T(8,128)(2,1)S(1)}, u32[]{:S(2)}, u32[]{:S(2)}) collective-permute-start(bf16[30,32,128]{2,1,0:T(8,128)(2,1)S(1)} %get-tuple-element.53), channel_id=1, source_target_pairs={{0,112},{16,32},{32,16},{48,64},{64,48},{80,96},{96,80},{112,0},{1... | collective-permute-start | bytes 737288 | tf_op jit(solution)/shard_map/ppermute | solution.py:675
  10.9 0.8 collective-permute-start.5
  11.7 2.8 %collective-permute-done.refs_0_.xb = bf16[60,16,128]{2,1,0:T(8,128)(2,1)S(1)} collective-permute-done((bf16[60,16,128]{2,1,0:T(8,128)(2,1)S(1)}, bf16[60,16,128]{2,1,0:T(8,128)(2,1)S(1)}, u32[]{:S(2)}, u32[]{:S(2)}) %collective-permute-start) | collective-permute-done | bytes 245792 | tf_op jit(solution)/shard_map/ppermute | solution.py:675
  14.5 1.5 %collective-permute-done.1.refs_1_.xa = bf16[60,16,128]{2,1,0:T(8,128)(2,1)S(1)} collective-permute-done((bf16[60,16,128]{2,1,0:T(8,128)(2,1)S(1)}, bf16[60,16,128]{2,1,0:T(8,128)(2,1)S(1)}, u32[]{:S(2)}, u32[]{:S(2)}) %collective-permute-start.1) | collective-permute-done | bytes 245792 | tf_op jit(solution)/shard_map/ppermute | solution.py:675
  15.9 0.3 shard_map.78
  16.2 0.1 collective-permute-start.2
  16.3 3.1 %collective-permute-start.3 = (bf16[26,32,128]{2,1,0:T(8,128)(2,1)S(1)}, bf16[26,32,128]{2,1,0:T(8,128)(2,1)S(1)}, u32[]{:S(2)}, u32[]{:S(2)}) collective-permute-start(bf16[26,32,128]{2,1,0:T(8,128)(2,1)S(1)} %get-tuple-element.50), channel_id=1, source_target_pairs={{0,112},{16,32},{32,16},{48,64},{64,48},{80,96},{96,80},{112,0},{1... | collective-permute-start | bytes 638984 | tf_op jit(solution)/shard_map/ppermute | solution.py:675
  19.4 2.7 %shard_map.80 = (f32[4,14,160,128]{3,2,1,0:T(8,128)S(1)}, f32[4,14,160,128]{3,2,1,0:T(8,128)S(1)}, f32[14,160,128]{2,1,0:T(8,128)S(1)}, f32[4,14,160,128]{3,2,1,...) custom-call(bf16[60,16,128]{2,1,0:T(8,128)(2,1)S(1)} %collective-permute-done.refs_0_.xb, ...), custom_call_target="tpu_custom_call" | custom-call | flops 4194304 | bytes 4194304 | tf_op jit(solution)/shard_map/pallas_call | solution.py:657
  22.2 0.8 collective-permute-done.3.cb
  23.0 4.9 %shard_map.81 = (f32[8,4,32,128]{3,2,1,0:T(8,128)S(1)}, f32[96,128]{1,0:T(8,128)S(1)}, bf16[96,128]{1,0:T(8,128)(2,1)S(1)}, f32[4,14,160,128]{3,2,1,0:T(8,128)S(...) custom-call(s32[8]{0:T(128)} %plan_far.7, ...), custom_call_target="tpu_custom_call", output_to_operand_aliasing={{3}: (4, {}), {4}: (5, {}), {5}: (6, {}), {6}: (7, {}), {7}... | custom-call | tf_op jit(solution)/shard_map/pallas_call | solution.py:657
  27.9 4.0 %collective-permute-start.11 = (bf16[96,128]{1,0:T(8,128)(2,1)S(1)}, bf16[96,128]{1,0:T(8,128)(2,1)S(1)}, u32[]{:S(2)}, u32[]{:S(2)}) collective-permute-start(bf16[96,128]{1,0:T(8,128)(2,1)S(1)} %get-tuple-element.67.rounded), channel_id=1, source_target_pairs={{0,15},{1,2},{2,1},{3,4},{4,3},{5,6},{6,5},{7,8},{8,7},{9,10},{10,... | collective-permute-start | bytes 73736 | tf_op jit(solution)/shard_map/ppermute | solution.py:675
  31.9 2.4 %collective-permute-start.9 = (bf16[96,128]{1,0:T(8,128)(2,1)S(1)}, bf16[96,128]{1,0:T(8,128)(2,1)S(1)}, u32[]{:S(2)}, u32[]{:S(2)}) collective-permute-start(bf16[96,128]{1,0:T(8,128)(2,1)S(1)} %get-tuple-element.67.rounded), channel_id=1, source_target_pairs={{0,112},{16,32},{32,16},{48,64},{64,48},{80,96},{96,80},{112,0},{1... | collective-permute-start | bytes 73736 | tf_op jit(solution)/shard_map/ppermute | solution.py:675
  34.4 0.8 collective-permute-done.11.xb
  35.1 0.6 collective-permute-done.10.xa
  35.7 0.6 collective-permute-done.9.tb
  36.4 0.3 shard_map.82
  36.7 2.8 %collective-permute-start.15 = (bf16[96,128]{1,0:T(8,128)(2,1)S(1)}, bf16[96,128]{1,0:T(8,128)(2,1)S(1)}, u32[]{:S(2)}, u32[]{:S(2)}) collective-permute-start(bf16[96,128]{1,0:T(8,128)(2,1)S(1)} %get-tuple-element.69.rounded), channel_id=1, source_target_pairs={{0,15},{1,2},{2,1},{3,4},{4,3},{5,6},{6,5},{7,8},{8,7},{9,10},{10,... | collective-permute-start | bytes 73736 | tf_op jit(solution)/shard_map/ppermute | solution.py:675
  39.5 1.3 %collective-permute-start.13 = (bf16[96,128]{1,0:T(8,128)(2,1)S(1)}, bf16[96,128]{1,0:T(8,128)(2,1)S(1)}, u32[]{:S(2)}, u32[]{:S(2)}) collective-permute-start(bf16[96,128]{1,0:T(8,128)(2,1)S(1)} %get-tuple-element.69.rounded), channel_id=1, source_target_pairs={{0,112},{16,32},{32,16},{48,64},{64,48},{80,96},{96,80},{112,0},{1... | collective-permute-start | bytes 73736 | tf_op jit(solution)/shard_map/ppermute | solution.py:675
  40.8 3.1 %collective-permute-done.15.xb = bf16[96,128]{1,0:T(8,128)(2,1)S(1)} collective-permute-done((bf16[96,128]{1,0:T(8,128)(2,1)S(1)}, bf16[96,128]{1,0:T(8,128)(2,1)S(1)}, u32[]{:S(2)}, u32[]{:S(2)}) %collective-permute-start.15) | collective-permute-done | bytes 24608 | tf_op jit(solution)/shard_map/ppermute | solution.py:675
  44.0 0.3 shard_map.83
  44.3 2.8 %collective-permute-start.19 = (bf16[96,128]{1,0:T(8,128)(2,1)S(1)}, bf16[96,128]{1,0:T(8,128)(2,1)S(1)}, u32[]{:S(2)}, u32[]{:S(2)}) collective-permute-start(bf16[96,128]{1,0:T(8,128)(2,1)S(1)} %get-tuple-element.71.rounded), channel_id=1, source_target_pairs={{0,15},{1,2},{2,1},{3,4},{4,3},{5,6},{6,5},{7,8},{8,7},{9,10},{10,... | collective-permute-start | bytes 73736 | tf_op jit(solution)/shard_map/ppermute | solution.py:675
  47.1 1.8 %collective-permute-start.17 = (bf16[96,128]{1,0:T(8,128)(2,1)S(1)}, bf16[96,128]{1,0:T(8,128)(2,1)S(1)}, u32[]{:S(2)}, u32[]{:S(2)}) collective-permute-start(bf16[96,128]{1,0:T(8,128)(2,1)S(1)} %get-tuple-element.71.rounded), channel_id=1, source_target_pairs={{0,112},{16,32},{32,16},{48,64},{64,48},{80,96},{96,80},{112,0},{1... | collective-permute-start | bytes 73736 | tf_op jit(solution)/shard_map/ppermute | solution.py:675
  48.9 2.6 %collective-permute-done.19.xb = bf16[96,128]{1,0:T(8,128)(2,1)S(1)} collective-permute-done((bf16[96,128]{1,0:T(8,128)(2,1)S(1)}, bf16[96,128]{1,0:T(8,128)(2,1)S(1)}, u32[]{:S(2)}, u32[]{:S(2)}) %collective-permute-start.19) | collective-permute-done | bytes 24608 | tf_op jit(solution)/shard_map/ppermute | solution.py:675
  51.5 0.3 shard_map.84
  51.9 2.8 %collective-permute-start.23 = (bf16[96,128]{1,0:T(8,128)(2,1)S(1)}, bf16[96,128]{1,0:T(8,128)(2,1)S(1)}, u32[]{:S(2)}, u32[]{:S(2)}) collective-permute-start(bf16[96,128]{1,0:T(8,128)(2,1)S(1)} %get-tuple-element.73.rounded), channel_id=1, source_target_pairs={{0,15},{1,2},{2,1},{3,4},{4,3},{5,6},{6,5},{7,8},{8,7},{9,10},{10,... | collective-permute-start | bytes 73736 | tf_op jit(solution)/shard_map/ppermute | solution.py:675
  54.6 1.0 %collective-permute-start.21 = (bf16[96,128]{1,0:T(8,128)(2,1)S(1)}, bf16[96,128]{1,0:T(8,128)(2,1)S(1)}, u32[]{:S(2)}, u32[]{:S(2)}) collective-permute-start(bf16[96,128]{1,0:T(8,128)(2,1)S(1)} %get-tuple-element.73.rounded), channel_id=1, source_target_pairs={{0,112},{16,32},{32,16},{48,64},{64,48},{80,96},{96,80},{112,0},{1... | collective-permute-start | bytes 73736 | tf_op jit(solution)/shard_map/ppermute | solution.py:675
  55.6 3.5 %collective-permute-done.23.xb = bf16[96,128]{1,0:T(8,128)(2,1)S(1)} collective-permute-done((bf16[96,128]{1,0:T(8,128)(2,1)S(1)}, bf16[96,128]{1,0:T(8,128)(2,1)S(1)}, u32[]{:S(2)}, u32[]{:S(2)}) %collective-permute-start.23) | collective-permute-done | bytes 24608 | tf_op jit(solution)/shard_map/ppermute | solution.py:675
  59.1 0.3 shard_map.85
  59.4 2.8 %collective-permute-start.27 = (bf16[96,128]{1,0:T(8,128)(2,1)S(1)}, bf16[96,128]{1,0:T(8,128)(2,1)S(1)}, u32[]{:S(2)}, u32[]{:S(2)}) collective-permute-start(bf16[96,128]{1,0:T(8,128)(2,1)S(1)} %get-tuple-element.75.rounded), channel_id=1, source_target_pairs={{0,15},{1,2},{2,1},{3,4},{4,3},{5,6},{6,5},{7,8},{8,7},{9,10},{10,... | collective-permute-start | bytes 73736 | tf_op jit(solution)/shard_map/ppermute | solution.py:675
  62.2 1.2 %collective-permute-start.25 = (bf16[96,128]{1,0:T(8,128)(2,1)S(1)}, bf16[96,128]{1,0:T(8,128)(2,1)S(1)}, u32[]{:S(2)}, u32[]{:S(2)}) collective-permute-start(bf16[96,128]{1,0:T(8,128)(2,1)S(1)} %get-tuple-element.75.rounded), channel_id=1, source_target_pairs={{0,112},{16,32},{32,16},{48,64},{64,48},{80,96},{96,80},{112,0},{1... | collective-permute-start | bytes 73736 | tf_op jit(solution)/shard_map/ppermute | solution.py:675
  63.5 3.2 %collective-permute-done.27.xb = bf16[96,128]{1,0:T(8,128)(2,1)S(1)} collective-permute-done((bf16[96,128]{1,0:T(8,128)(2,1)S(1)}, bf16[96,128]{1,0:T(8,128)(2,1)S(1)}, u32[]{:S(2)}, u32[]{:S(2)}) %collective-permute-start.27) | collective-permute-done | bytes 24608 | tf_op jit(solution)/shard_map/ppermute | solution.py:675
  66.7 2.0 %shard_map.86 = (f32[8,4,32,128]{3,2,1,0:T(8,128)S(1)}, bf16[48,16,128]{2,1,0:T(8,128)(2,1)S(1)}, bf16[48,16,128]{2,1,0:T(8,128)(2,1)S(1)}) custom-call(f32[7,6,48,128]{3,2,1,0:T(8,128)S(1)} %get-tuple-element.65.operator, f32[96,128]{1,0:T(8,128)S(1)} %get-tuple-element.66.rhs.estimate, f32[96,128]{1,0:T(8,128)S(1)} %get-tuple-element.74.estimate, ...), custom_call_target="tpu_custom_call" | custom-call | tf_op jit(solution)/shard_map/pallas_call | solution.py:657
  68.7 0.1 shard_map.87
  68.8 1.3 %collective-permute-start.30 = (bf16[20,32,128]{2,1,0:T(8,128)(2,1)S(1)}, bf16[20,32,128]{2,1,0:T(8,128)(2,1)S(1)}, u32[]{:S(2)}, u32[]{:S(2)}) collective-permute-start(bf16[20,32,128]{2,1,0:T(8,128)(2,1)S(1)} %get-tuple-element.80), channel_id=1, source_target_pairs={{0,112},{16,32},{32,16},{48,64},{64,48},{80,96},{96,80},{112,0},{1... | collective-permute-start | bytes 491528 | tf_op jit(solution)/shard_map/ppermute | solution.py:675
  70.1 2.7 %collective-permute-start.28 = (bf16[48,16,128]{2,1,0:T(8,128)(2,1)S(1)}, bf16[48,16,128]{2,1,0:T(8,128)(2,1)S(1)}, u32[]{:S(2)}, u32[]{:S(2)}) collective-permute-start(bf16[48,16,128]{2,1,0:T(8,128)(2,1)S(1)} %get-tuple-element.77), channel_id=1, source_target_pairs={{0,15},{1,2},{2,1},{3,4},{4,3},{5,6},{6,5},{7,8},{8,7},{9,10},{10,... | collective-permute-start | bytes 589832 | tf_op jit(solution)/shard_map/ppermute | solution.py:675
  72.8 1.5 %collective-permute-start.31 = (bf16[20,32,128]{2,1,0:T(8,128)(2,1)S(1)}, bf16[20,32,128]{2,1,0:T(8,128)(2,1)S(1)}, u32[]{:S(2)}, u32[]{:S(2)}) collective-permute-start(bf16[20,32,128]{2,1,0:T(8,128)(2,1)S(1)} %get-tuple-element.81), channel_id=1, source_target_pairs={{0,112},{16,32},{32,16},{48,64},{64,48},{80,96},{96,80},{112,0},{1... | collective-permute-start | bytes 491528 | tf_op jit(solution)/shard_map/ppermute | solution.py:675
  74.2 0.6 collective-permute-done.30.tb2.refs_5_
  74.8 3.9 %collective-permute-done.31.tb1.refs_4_ = bf16[20,32,128]{2,1,0:T(8,128)(2,1)S(1)} collective-permute-done((bf16[20,32,128]{2,1,0:T(8,128)(2,1)S(1)}, bf16[20,32,128]{2,1,0:T(8,128)(2,1)S(1)}, u32[]{:S(2)}, u32[]{:S(2)}) %collective-permute-start.31) | collective-permute-done | bytes 163872 | tf_op jit(solution)/shard_map/ppermute | solution.py:675
  78.7 0.4 collective-permute-done.28.xb.refs_0_
  79.1 0.2 shard_map.89
  79.4 0.1 collective-permute-start.34
  79.5 2.0 %collective-permute-start.35 = (bf16[32,32,128]{2,1,0:T(8,128)(2,1)S(1)}, bf16[32,32,128]{2,1,0:T(8,128)(2,1)S(1)}, u32[]{:S(2)}, u32[]{:S(2)}) collective-permute-start(bf16[32,32,128]{2,1,0:T(8,128)(2,1)S(1)} %get-tuple-element.87), channel_id=1, source_target_pairs={{0,112},{16,32},{32,16},{48,64},{64,48},{80,96},{96,80},{112,0},{1... | collective-permute-start | bytes 786440 | tf_op jit(solution)/shard_map/ppermute | solution.py:675
  81.5 1.5 %shard_map.88 = (f32[4,14,160,128]{3,2,1,0:T(8,128)S(1)}, f32[4,14,160,128]{3,2,1,0:T(8,128)S(1)}) custom-call(bf16[48,16,128]{2,1,0:T(8,128)(2,1)S(1)} %collective-permute-done.28.xb.refs_0_, bf16[48,16,128]{2,1,0:T(8,128)(2,1)S(1)} %collective-permute-done.29.xa.refs_1_, bf16[20,32,128]{2,1,0:T(8,128)(2,1)S(1)} %collective-permute-done.30.tb2.refs_5_, ...), custom_call_target="tpu_custom_call" | custom-call | flops 4194304 | bytes 4194304 | tf_op jit(solution)/shard_map/pallas_call | solution.py:657
  83.0 3.5 %collective-permute-done.35.cb = bf16[32,32,128]{2,1,0:T(8,128)(2,1)S(1)} collective-permute-done((bf16[32,32,128]{2,1,0:T(8,128)(2,1)S(1)}, bf16[32,32,128]{2,1,0:T(8,128)(2,1)S(1)}, u32[]{:S(2)}, u32[]{:S(2)}) %collective-permute-start.35) | collective-permute-done | bytes 262176 | tf_op jit(solution)/shard_map/ppermute | solution.py:675
  86.5 5.7 %shard_map.90 = (f32[8,4,32,128]{3,2,1,0:T(8,128)}, f32[8,4,32,128]{3,2,1,0:T(8,128)}, f32[4,14,160,128]{3,2,1,0:T(8,128)S(1)}, f32[4,14,160,128]{3,2,1,0:T(8,128)S(1)}) custom-call(s32[8]{0:T(128)} %plan_far.7, f32[4,32,128]{2,1,0:T(8,128)S(1)} %get-tuple-element.46.mass, ...), custom_call_target="tpu_custom_call", output_to_operand_aliasing={{2}: (5, {}), {3}: (6, {})} | custom-call | tf_op jit(solution)/shard_map/pallas_call | solution.py:657
  (40 shorter events, 0.1 us)
Async XLA Ops:
  0.6 22.3 %copy-start = (bf16[24,4,4,8,4,128]{5,4,3,2,1,0:T(4,128)(2,1)S(1)}, bf16[24,4,4,8,4,128]{5,4,3,2,1,0:T(4,128)(2,1)}, u32[]{:S(2)}) copy-start(bf16[24,4,4,8,4,128]{5,4,3,2,1,0:T(4,128)(2,1)} %param.9) | copy-start | bytes 9437188
  2.1 12.3 %collective-permute-start = (bf16[60,16,128]{2,1,0:T(8,128)(2,1)S(1)}, bf16[60,16,128]{2,1,0:T(8,128)(2,1)S(1)}, u32[]{:S(2)}, u32[]{:S(2)}) collective-permute-start(bf16[60,16,128]{2,1,0:T(8,128)(2,1)S(1)} %get-tuple-element.47), channel_id=1, source_target_pairs={{0,15},{1,2},{2,1},{3,4},{4,3},{5,6},{6,5},{7,8},{8,7},{9,10},{10,... | collective-permute-start | bytes 737288 | tf_op jit(solution)/shard_map/ppermute | solution.py:675
  8.5 7.4 %collective-permute-start.1 = (bf16[60,16,128]{2,1,0:T(8,128)(2,1)S(1)}, bf16[60,16,128]{2,1,0:T(8,128)(2,1)S(1)}, u32[]{:S(2)}, u32[]{:S(2)}) collective-permute-start(bf16[60,16,128]{2,1,0:T(8,128)(2,1)S(1)} %get-tuple-element.48), channel_id=1, source_target_pairs={{0,1},{1,0},{2,3},{3,2},{4,5},{5,4},{6,7},{7,6},{8,9},{9,8},{10,11... | collective-permute-start | bytes 737288 | tf_op jit(solution)/shard_map/ppermute | solution.py:675
  8.6 7.7 %collective-permute-start.4 = (bf16[30,32,128]{2,1,0:T(8,128)(2,1)S(1)}, bf16[30,32,128]{2,1,0:T(8,128)(2,1)S(1)}, u32[]{:S(2)}, u32[]{:S(2)}) collective-permute-start(bf16[30,32,128]{2,1,0:T(8,128)(2,1)S(1)} %get-tuple-element.53), channel_id=1, source_target_pairs={{0,112},{16,32},{32,16},{48,64},{64,48},{80,96},{96,80},{112,0},{1... | collective-permute-start | bytes 737288 | tf_op jit(solution)/shard_map/ppermute | solution.py:675
  10.9 8.5 %collective-permute-start.5 = (bf16[30,32,128]{2,1,0:T(8,128)(2,1)S(1)}, bf16[30,32,128]{2,1,0:T(8,128)(2,1)S(1)}, u32[]{:S(2)}, u32[]{:S(2)}) collective-permute-start(bf16[30,32,128]{2,1,0:T(8,128)(2,1)S(1)} %get-tuple-element.54), channel_id=1, source_target_pairs={{0,112},{16,32},{32,16},{48,64},{64,48},{80,96},{96,80},{112,0},{1... | collective-permute-start | bytes 737288 | tf_op jit(solution)/shard_map/ppermute | solution.py:675
  11.7 7.8 %collective-permute-start.6 = (bf16[30,32,128]{2,1,0:T(8,128)(2,1)S(1)}, bf16[30,32,128]{2,1,0:T(8,128)(2,1)S(1)}, u32[]{:S(2)}, u32[]{:S(2)}) collective-permute-start(bf16[30,32,128]{2,1,0:T(8,128)(2,1)S(1)} %get-tuple-element.55), channel_id=1, source_target_pairs={{0,16},{16,0},{32,48},{48,32},{64,80},{80,64},{96,112},{112,96},{1... | collective-permute-start | bytes 737288 | tf_op jit(solution)/shard_map/ppermute | solution.py:675
  14.5 5.0 %collective-permute-start.7 = (bf16[30,32,128]{2,1,0:T(8,128)(2,1)S(1)}, bf16[30,32,128]{2,1,0:T(8,128)(2,1)S(1)}, u32[]{:S(2)}, u32[]{:S(2)}) collective-permute-start(bf16[30,32,128]{2,1,0:T(8,128)(2,1)S(1)} %get-tuple-element.56), channel_id=1, source_target_pairs={{0,16},{16,0},{32,48},{48,32},{64,80},{80,64},{96,112},{112,96},{1... | collective-permute-start | bytes 737288 | tf_op jit(solution)/shard_map/ppermute | solution.py:675
  16.2 6.0 %collective-permute-start.2 = (bf16[26,32,128]{2,1,0:T(8,128)(2,1)S(1)}, bf16[26,32,128]{2,1,0:T(8,128)(2,1)S(1)}, u32[]{:S(2)}, u32[]{:S(2)}) collective-permute-start(bf16[26,32,128]{2,1,0:T(8,128)(2,1)S(1)} %get-tuple-element.49), channel_id=1, source_target_pairs={{0,16},{16,0},{32,48},{48,32},{64,80},{80,64},{96,112},{112,96},{1... | collective-permute-start | bytes 638984 | tf_op jit(solution)/shard_map/ppermute | solution.py:675
  16.3 6.6 %collective-permute-start.3 = (bf16[26,32,128]{2,1,0:T(8,128)(2,1)S(1)}, bf16[26,32,128]{2,1,0:T(8,128)(2,1)S(1)}, u32[]{:S(2)}, u32[]{:S(2)}) collective-permute-start(bf16[26,32,128]{2,1,0:T(8,128)(2,1)S(1)} %get-tuple-element.50), channel_id=1, source_target_pairs={{0,112},{16,32},{32,16},{48,64},{64,48},{80,96},{96,80},{112,0},{1... | collective-permute-start | bytes 638984 | tf_op jit(solution)/shard_map/ppermute | solution.py:675
  27.9 7.2 %collective-permute-start.11 = (bf16[96,128]{1,0:T(8,128)(2,1)S(1)}, bf16[96,128]{1,0:T(8,128)(2,1)S(1)}, u32[]{:S(2)}, u32[]{:S(2)}) collective-permute-start(bf16[96,128]{1,0:T(8,128)(2,1)S(1)} %get-tuple-element.67.rounded), channel_id=1, source_target_pairs={{0,15},{1,2},{2,1},{3,4},{4,3},{5,6},{6,5},{7,8},{8,7},{9,10},{10,... | collective-permute-start | bytes 73736 | tf_op jit(solution)/shard_map/ppermute | solution.py:675
  31.9 3.8 %collective-permute-start.10 = (bf16[96,128]{1,0:T(8,128)(2,1)S(1)}, bf16[96,128]{1,0:T(8,128)(2,1)S(1)}, u32[]{:S(2)}, u32[]{:S(2)}) collective-permute-start(bf16[96,128]{1,0:T(8,128)(2,1)S(1)} %get-tuple-element.67.rounded), channel_id=1, source_target_pairs={{0,1},{1,0},{2,3},{3,2},{4,5},{5,4},{6,7},{7,6},{8,9},{9,8},{10,11... | collective-permute-start | bytes 73736 | tf_op jit(solution)/shard_map/ppermute | solution.py:675
  31.9 4.5 %collective-permute-start.9 = (bf16[96,128]{1,0:T(8,128)(2,1)S(1)}, bf16[96,128]{1,0:T(8,128)(2,1)S(1)}, u32[]{:S(2)}, u32[]{:S(2)}) collective-permute-start(bf16[96,128]{1,0:T(8,128)(2,1)S(1)} %get-tuple-element.67.rounded), channel_id=1, source_target_pairs={{0,112},{16,32},{32,16},{48,64},{64,48},{80,96},{96,80},{112,0},{1... | collective-permute-start | bytes 73736 | tf_op jit(solution)/shard_map/ppermute | solution.py:675
  34.4 2.0 %collective-permute-start.8 = (bf16[96,128]{1,0:T(8,128)(2,1)S(1)}, bf16[96,128]{1,0:T(8,128)(2,1)S(1)}, u32[]{:S(2)}, u32[]{:S(2)}) collective-permute-start(bf16[96,128]{1,0:T(8,128)(2,1)S(1)} %get-tuple-element.67.rounded), channel_id=1, source_target_pairs={{0,16},{16,0},{32,48},{48,32},{64,80},{80,64},{96,112},{112,96},{1... | collective-permute-start | bytes 73736 | tf_op jit(solution)/shard_map/ppermute | solution.py:675
  36.7 7.2 %collective-permute-start.15 = (bf16[96,128]{1,0:T(8,128)(2,1)S(1)}, bf16[96,128]{1,0:T(8,128)(2,1)S(1)}, u32[]{:S(2)}, u32[]{:S(2)}) collective-permute-start(bf16[96,128]{1,0:T(8,128)(2,1)S(1)} %get-tuple-element.69.rounded), channel_id=1, source_target_pairs={{0,15},{1,2},{2,1},{3,4},{4,3},{5,6},{6,5},{7,8},{8,7},{9,10},{10,... | collective-permute-start | bytes 73736 | tf_op jit(solution)/shard_map/ppermute | solution.py:675
  39.5 4.5 %collective-permute-start.14 = (bf16[96,128]{1,0:T(8,128)(2,1)S(1)}, bf16[96,128]{1,0:T(8,128)(2,1)S(1)}, u32[]{:S(2)}, u32[]{:S(2)}) collective-permute-start(bf16[96,128]{1,0:T(8,128)(2,1)S(1)} %get-tuple-element.69.rounded), channel_id=1, source_target_pairs={{0,1},{1,0},{2,3},{3,2},{4,5},{5,4},{6,7},{7,6},{8,9},{9,8},{10,11... | collective-permute-start | bytes 73736 | tf_op jit(solution)/shard_map/ppermute | solution.py:675
  39.5 4.5 %collective-permute-start.13 = (bf16[96,128]{1,0:T(8,128)(2,1)S(1)}, bf16[96,128]{1,0:T(8,128)(2,1)S(1)}, u32[]{:S(2)}, u32[]{:S(2)}) collective-permute-start(bf16[96,128]{1,0:T(8,128)(2,1)S(1)} %get-tuple-element.69.rounded), channel_id=1, source_target_pairs={{0,112},{16,32},{32,16},{48,64},{64,48},{80,96},{96,80},{112,0},{1... | collective-permute-start | bytes 73736 | tf_op jit(solution)/shard_map/ppermute | solution.py:675
  40.8 3.2 %collective-permute-start.12 = (bf16[96,128]{1,0:T(8,128)(2,1)S(1)}, bf16[96,128]{1,0:T(8,128)(2,1)S(1)}, u32[]{:S(2)}, u32[]{:S(2)}) collective-permute-start(bf16[96,128]{1,0:T(8,128)(2,1)S(1)} %get-tuple-element.69.rounded), channel_id=1, source_target_pairs={{0,16},{16,0},{32,48},{48,32},{64,80},{80,64},{96,112},{112,96},{1... | collective-permute-start | bytes 73736 | tf_op jit(solution)/shard_map/ppermute | solution.py:675
  44.3 7.2 %collective-permute-start.19 = (bf16[96,128]{1,0:T(8,128)(2,1)S(1)}, bf16[96,128]{1,0:T(8,128)(2,1)S(1)}, u32[]{:S(2)}, u32[]{:S(2)}) collective-permute-start(bf16[96,128]{1,0:T(8,128)(2,1)S(1)} %get-tuple-element.71.rounded), channel_id=1, source_target_pairs={{0,15},{1,2},{2,1},{3,4},{4,3},{5,6},{6,5},{7,8},{8,7},{9,10},{10,... | collective-permute-start | bytes 73736 | tf_op jit(solution)/shard_map/ppermute | solution.py:675
  47.1 4.5 %collective-permute-start.18 = (bf16[96,128]{1,0:T(8,128)(2,1)S(1)}, bf16[96,128]{1,0:T(8,128)(2,1)S(1)}, u32[]{:S(2)}, u32[]{:S(2)}) collective-permute-start(bf16[96,128]{1,0:T(8,128)(2,1)S(1)} %get-tuple-element.71.rounded), channel_id=1, source_target_pairs={{0,1},{1,0},{2,3},{3,2},{4,5},{5,4},{6,7},{7,6},{8,9},{9,8},{10,11... | collective-permute-start | bytes 73736 | tf_op jit(solution)/shard_map/ppermute | solution.py:675
  47.1 4.5 %collective-permute-start.17 = (bf16[96,128]{1,0:T(8,128)(2,1)S(1)}, bf16[96,128]{1,0:T(8,128)(2,1)S(1)}, u32[]{:S(2)}, u32[]{:S(2)}) collective-permute-start(bf16[96,128]{1,0:T(8,128)(2,1)S(1)} %get-tuple-element.71.rounded), channel_id=1, source_target_pairs={{0,112},{16,32},{32,16},{48,64},{64,48},{80,96},{96,80},{112,0},{1... | collective-permute-start | bytes 73736 | tf_op jit(solution)/shard_map/ppermute | solution.py:675
  48.9 2.6 %collective-permute-start.16 = (bf16[96,128]{1,0:T(8,128)(2,1)S(1)}, bf16[96,128]{1,0:T(8,128)(2,1)S(1)}, u32[]{:S(2)}, u32[]{:S(2)}) collective-permute-start(bf16[96,128]{1,0:T(8,128)(2,1)S(1)} %get-tuple-element.71.rounded), channel_id=1, source_target_pairs={{0,16},{16,0},{32,48},{48,32},{64,80},{80,64},{96,112},{112,96},{1... | collective-permute-start | bytes 73736 | tf_op jit(solution)/shard_map/ppermute | solution.py:675
  51.9 7.2 %collective-permute-start.23 = (bf16[96,128]{1,0:T(8,128)(2,1)S(1)}, bf16[96,128]{1,0:T(8,128)(2,1)S(1)}, u32[]{:S(2)}, u32[]{:S(2)}) collective-permute-start(bf16[96,128]{1,0:T(8,128)(2,1)S(1)} %get-tuple-element.73.rounded), channel_id=1, source_target_pairs={{0,15},{1,2},{2,1},{3,4},{4,3},{5,6},{6,5},{7,8},{8,7},{9,10},{10,... | collective-permute-start | bytes 73736 | tf_op jit(solution)/shard_map/ppermute | solution.py:675
  54.6 4.5 %collective-permute-start.22 = (bf16[96,128]{1,0:T(8,128)(2,1)S(1)}, bf16[96,128]{1,0:T(8,128)(2,1)S(1)}, u32[]{:S(2)}, u32[]{:S(2)}) collective-permute-start(bf16[96,128]{1,0:T(8,128)(2,1)S(1)} %get-tuple-element.73.rounded), channel_id=1, source_target_pairs={{0,1},{1,0},{2,3},{3,2},{4,5},{5,4},{6,7},{7,6},{8,9},{9,8},{10,11... | collective-permute-start | bytes 73736 | tf_op jit(solution)/shard_map/ppermute | solution.py:675
  54.6 4.5 %collective-permute-start.21 = (bf16[96,128]{1,0:T(8,128)(2,1)S(1)}, bf16[96,128]{1,0:T(8,128)(2,1)S(1)}, u32[]{:S(2)}, u32[]{:S(2)}) collective-permute-start(bf16[96,128]{1,0:T(8,128)(2,1)S(1)} %get-tuple-element.73.rounded), channel_id=1, source_target_pairs={{0,112},{16,32},{32,16},{48,64},{64,48},{80,96},{96,80},{112,0},{1... | collective-permute-start | bytes 73736 | tf_op jit(solution)/shard_map/ppermute | solution.py:675
  55.6 3.5 %collective-permute-start.20 = (bf16[96,128]{1,0:T(8,128)(2,1)S(1)}, bf16[96,128]{1,0:T(8,128)(2,1)S(1)}, u32[]{:S(2)}, u32[]{:S(2)}) collective-permute-start(bf16[96,128]{1,0:T(8,128)(2,1)S(1)} %get-tuple-element.73.rounded), channel_id=1, source_target_pairs={{0,16},{16,0},{32,48},{48,32},{64,80},{80,64},{96,112},{112,96},{1... | collective-permute-start | bytes 73736 | tf_op jit(solution)/shard_map/ppermute | solution.py:675
  59.4 7.2 %collective-permute-start.27 = (bf16[96,128]{1,0:T(8,128)(2,1)S(1)}, bf16[96,128]{1,0:T(8,128)(2,1)S(1)}, u32[]{:S(2)}, u32[]{:S(2)}) collective-permute-start(bf16[96,128]{1,0:T(8,128)(2,1)S(1)} %get-tuple-element.75.rounded), channel_id=1, source_target_pairs={{0,15},{1,2},{2,1},{3,4},{4,3},{5,6},{6,5},{7,8},{8,7},{9,10},{10,... | collective-permute-start | bytes 73736 | tf_op jit(solution)/shard_map/ppermute | solution.py:675
  62.2 4.5 %collective-permute-start.26 = (bf16[96,128]{1,0:T(8,128)(2,1)S(1)}, bf16[96,128]{1,0:T(8,128)(2,1)S(1)}, u32[]{:S(2)}, u32[]{:S(2)}) collective-permute-start(bf16[96,128]{1,0:T(8,128)(2,1)S(1)} %get-tuple-element.75.rounded), channel_id=1, source_target_pairs={{0,1},{1,0},{2,3},{3,2},{4,5},{5,4},{6,7},{7,6},{8,9},{9,8},{10,11... | collective-permute-start | bytes 73736 | tf_op jit(solution)/shard_map/ppermute | solution.py:675
  62.2 4.5 %collective-permute-start.25 = (bf16[96,128]{1,0:T(8,128)(2,1)S(1)}, bf16[96,128]{1,0:T(8,128)(2,1)S(1)}, u32[]{:S(2)}, u32[]{:S(2)}) collective-permute-start(bf16[96,128]{1,0:T(8,128)(2,1)S(1)} %get-tuple-element.75.rounded), channel_id=1, source_target_pairs={{0,112},{16,32},{32,16},{48,64},{64,48},{80,96},{96,80},{112,0},{1... | collective-permute-start | bytes 73736 | tf_op jit(solution)/shard_map/ppermute | solution.py:675
  63.5 3.2 %collective-permute-start.24 = (bf16[96,128]{1,0:T(8,128)(2,1)S(1)}, bf16[96,128]{1,0:T(8,128)(2,1)S(1)}, u32[]{:S(2)}, u32[]{:S(2)}) collective-permute-start(bf16[96,128]{1,0:T(8,128)(2,1)S(1)} %get-tuple-element.75.rounded), channel_id=1, source_target_pairs={{0,16},{16,0},{32,48},{48,32},{64,80},{80,64},{96,112},{112,96},{1... | collective-permute-start | bytes 73736 | tf_op jit(solution)/shard_map/ppermute | solution.py:675
  68.8 6.0 %collective-permute-start.30 = (bf16[20,32,128]{2,1,0:T(8,128)(2,1)S(1)}, bf16[20,32,128]{2,1,0:T(8,128)(2,1)S(1)}, u32[]{:S(2)}, u32[]{:S(2)}) collective-permute-start(bf16[20,32,128]{2,1,0:T(8,128)(2,1)S(1)} %get-tuple-element.80), channel_id=1, source_target_pairs={{0,112},{16,32},{32,16},{48,64},{64,48},{80,96},{96,80},{112,0},{1... | collective-permute-start | bytes 491528 | tf_op jit(solution)/shard_map/ppermute | solution.py:675
  70.1 9.0 %collective-permute-start.28 = (bf16[48,16,128]{2,1,0:T(8,128)(2,1)S(1)}, bf16[48,16,128]{2,1,0:T(8,128)(2,1)S(1)}, u32[]{:S(2)}, u32[]{:S(2)}) collective-permute-start(bf16[48,16,128]{2,1,0:T(8,128)(2,1)S(1)} %get-tuple-element.77), channel_id=1, source_target_pairs={{0,15},{1,2},{2,1},{3,4},{4,3},{5,6},{6,5},{7,8},{8,7},{9,10},{10,... | collective-permute-start | bytes 589832 | tf_op jit(solution)/shard_map/ppermute | solution.py:675
  72.8 6.3 %collective-permute-start.29 = (bf16[48,16,128]{2,1,0:T(8,128)(2,1)S(1)}, bf16[48,16,128]{2,1,0:T(8,128)(2,1)S(1)}, u32[]{:S(2)}, u32[]{:S(2)}) collective-permute-start(bf16[48,16,128]{2,1,0:T(8,128)(2,1)S(1)} %get-tuple-element.78), channel_id=1, source_target_pairs={{0,1},{1,0},{2,3},{3,2},{4,5},{5,4},{6,7},{7,6},{8,9},{9,8},{10,11... | collective-permute-start | bytes 589832 | tf_op jit(solution)/shard_map/ppermute | solution.py:675
  72.8 6.0 %collective-permute-start.31 = (bf16[20,32,128]{2,1,0:T(8,128)(2,1)S(1)}, bf16[20,32,128]{2,1,0:T(8,128)(2,1)S(1)}, u32[]{:S(2)}, u32[]{:S(2)}) collective-permute-start(bf16[20,32,128]{2,1,0:T(8,128)(2,1)S(1)} %get-tuple-element.81), channel_id=1, source_target_pairs={{0,112},{16,32},{32,16},{48,64},{64,48},{80,96},{96,80},{112,0},{1... | collective-permute-start | bytes 491528 | tf_op jit(solution)/shard_map/ppermute | solution.py:675
  74.2 4.5 %collective-permute-start.32 = (bf16[20,32,128]{2,1,0:T(8,128)(2,1)S(1)}, bf16[20,32,128]{2,1,0:T(8,128)(2,1)S(1)}, u32[]{:S(2)}, u32[]{:S(2)}) collective-permute-start(bf16[20,32,128]{2,1,0:T(8,128)(2,1)S(1)} %get-tuple-element.82), channel_id=1, source_target_pairs={{0,16},{16,0},{32,48},{48,32},{64,80},{80,64},{96,112},{112,96},{1... | collective-permute-start | bytes 491528 | tf_op jit(solution)/shard_map/ppermute | solution.py:675
  74.8 3.9 %collective-permute-start.33 = (bf16[20,32,128]{2,1,0:T(8,128)(2,1)S(1)}, bf16[20,32,128]{2,1,0:T(8,128)(2,1)S(1)}, u32[]{:S(2)}, u32[]{:S(2)}) collective-permute-start(bf16[20,32,128]{2,1,0:T(8,128)(2,1)S(1)} %get-tuple-element.83), channel_id=1, source_target_pairs={{0,16},{16,0},{32,48},{48,32},{64,80},{80,64},{96,112},{112,96},{1... | collective-permute-start | bytes 491528 | tf_op jit(solution)/shard_map/ppermute | solution.py:675
  79.4 3.7 %collective-permute-start.34 = (bf16[32,32,128]{2,1,0:T(8,128)(2,1)S(1)}, bf16[32,32,128]{2,1,0:T(8,128)(2,1)S(1)}, u32[]{:S(2)}, u32[]{:S(2)}) collective-permute-start(bf16[32,32,128]{2,1,0:T(8,128)(2,1)S(1)} %get-tuple-element.86), channel_id=1, source_target_pairs={{0,16},{16,0},{32,48},{48,32},{64,80},{80,64},{96,112},{112,96},{1... | collective-permute-start | bytes 786440 | tf_op jit(solution)/shard_map/ppermute | solution.py:675
  79.5 7.1 %collective-permute-start.35 = (bf16[32,32,128]{2,1,0:T(8,128)(2,1)S(1)}, bf16[32,32,128]{2,1,0:T(8,128)(2,1)S(1)}, u32[]{:S(2)}, u32[]{:S(2)}) collective-permute-start(bf16[32,32,128]{2,1,0:T(8,128)(2,1)S(1)} %get-tuple-element.87), channel_id=1, source_target_pairs={{0,112},{16,32},{32,16},{48,64},{64,48},{80,96},{96,80},{112,0},{1... | collective-permute-start | bytes 786440 | tf_op jit(solution)/shard_map/ppermute | solution.py:675
where the time goes:
time: 93 us; the launch traced here: 92.4 us
  starting transfers between devices  43.2 us (46%)
  waiting for transfers between devices  27.9 us (30%)
  Pallas kernels  20.4 us (22%)
  between operations  0.96 us (1%)
    ppermute x36, starting transfers between devices, swap(): return lax.ppermute(values, axis, pairs)  43.2 us
    ppermute x36, waiting for transfers between devices, swap(): return lax.ppermute(values, axis, pairs)  27.9 us
    pallas_call x14, Pallas kernels, call(): pl.pallas_call(kernel, out_shape=outs, in_specs=specs, out_specs=[VM] * l...  20.4 us
  transfers between devices with their start and end apart: 36, of which 14 were waited for; matrix products, arithmetic and copies ran while one was open for 0% of the time, Pallas kernels for 5%

commit v1 on v0

--- a/solution.py
+++ b/solution.py
@@ -444,7 +444,7 @@
 
 def pre_kernel(
     plan_far, mass, ca, cb, src_in, signs_in, inverse_in, field_a_in, field_b_in, near_null,
-    out_solution, out_rhs, out_rounded, src, signs, inverse, field_a, field_b,
+    out_solution, out_rhs, out_rounded, out_sent, src, signs, inverse, field_a, field_b,
     diag, resid, sums, plan, sem,
 ):
     del src_in, signs_in, inverse_in, field_a_in, field_b_in
@@ -504,17 +504,39 @@
     rhs = exact_sum(spread, exact_sum(fold, sums[...], True), False)
     out_rhs[...] = rhs
     out_rounded[...] = rhs.astype(BF16)
+    out_sent[...] = compact(rhs, lane >> 5)
+
+
+def compact(values, group):
+    tiles = [values[8 * i : 8 * i + 8] for i in range(12)]
+    parts = []
+    for first in (0, 4, 8):
+        value = tiles[first]
+        for g in range(1, 4):
+            value = jnp.where(group == g, tiles[first + g], value)
+        parts.append(value)
+    return jnp.concatenate(parts + [jnp.zeros_like(parts[0])], 0).astype(BF16)
+
+
+def expand(data, group):
+    values = data.astype(F32)
+    tiles = []
+    for i in range(12):
+        value = jnp.where(group == i % 4, values[8 * (i // 4) : 8 * (i // 4) + 8], 0.0)
+        value = value + roll(value, 64, 1)
+        tiles.append(value + roll(value, 32, 1))
+    return tiles
 
 
 def coarse_step(operator, rhs, estimate, rounded, ta, tb, xa, xb, beside, out):
     row, lane = tile_iotas()
     t_odd, x_odd = lax.axis_index("ta") & 1, lax.axis_index("xyz") & 1
     even_row = (row & 1) == 0
+    ta, tb, xa, xb = (expand(data[...], lane >> 5) for data in (ta, tb, xa, xb))
     for i in range(12):
         where = slice(8 * i, 8 * i + 8)
         own = rounded[where].astype(F32)
-        t_first, t_second = ta[where].astype(F32), tb[where].astype(F32)
-        x_first, x_second = xa[where].astype(F32), xb[where].astype(F32)
+        t_first, t_second, x_first, x_second = ta[i], tb[i], xa[i], xb[i]
         beside[0, where] = own
         beside[1, where] = jnp.where(t_odd == 0, t_first, t_second)
         beside[2, where] = jnp.where(t_odd == 0, t_second, t_first)
@@ -547,9 +569,10 @@
             out[where] = estimate[where] + (rhs[where] - value)
 
 
-def coarse_kernel(operator, rhs, estimate, rounded, ta, tb, xa, xb, out, out_rounded, beside):
+def coarse_kernel(operator, rhs, estimate, rounded, ta, tb, xa, xb, out, out_rounded, out_sent, beside):
     coarse_step(operator, rhs, estimate, rounded, ta, tb, xa, xb, beside, out)
     out_rounded[...] = out[...].astype(BF16)
+    out_sent[...] = compact(out[...], tile_iotas()[1] >> 5)
 
 
 def prolong_kernel(
@@ -736,23 +759,24 @@
         far=(9, 10),
         cost=1 << 22,
     )
-    solution, rhs, rounded, src, signs, inverse, *_ = call(
+    solution, rhs, rounded, sent, src, signs, inverse, *_ = call(
         pre_kernel,
         12,
-        [shape(field, F32), shape((count, LANES), F32), shape((count, LANES), BF16)] + inputs + [shape(ext, F32)] * 2,
+        [shape(field, F32), shape((count, LANES), F32), shape((count, LANES), BF16), shape((32, LANES), BF16)]
+        + inputs + [shape(ext, F32)] * 2,
         [(LT, 2 * ROWS, LANES), own, (8 * count, LANES), pltpu.SMEM((SWEEPS,), I32), pltpu.SemaphoreType.DMA],
         plan, mass, *corners, *inputs_near, near_null,
-        aliases=((4, 3), (5, 4), (6, 5), (7, 6), (8, 7)),
+        aliases=((4, 4), (5, 5), (6, 6), (7, 7), (8, 8)),
         far=(0,),
     )
     estimate = rhs
     beside = (7, count, LANES)
     for turn in range(1, KC):
-        near = swap_four(rounded, rounded, rounded, rounded)
+        near = swap_four(sent, sent, sent, sent)
         given = (operator, rhs, estimate, rounded, *near)
         if turn < KC - 1:
-            outs = [shape((count, LANES), F32), shape((count, LANES), BF16)]
-            estimate, rounded = call(coarse_kernel, 6, outs, [beside], *given)
+            outs = [shape((count, LANES), F32), shape((count, LANES), BF16), shape((32, LANES), BF16)]
+            estimate, rounded, sent = call(coarse_kernel, 6, outs, [beside], *given)
     solution, x_a, x_b = call(
         prolong_kernel,
         12,

time: 93 us -> 92.6 us (level)
  no operation moved by 1% of the time
where the time goes in v1:
time: 92.6 us; the launch traced here: 92 us
  starting transfers between devices  43.1 us (47%)
  waiting for transfers between devices  27 us (29%)
  Pallas kernels  20.9 us (23%)
  between operations  0.98 us (1%)
    ppermute x36, starting transfers between devices, swap(): return lax.ppermute(values, axis, pairs)  43.1 us
    ppermute x36, waiting for transfers between devices, swap(): return lax.ppermute(values, axis, pairs)  27 us
    pallas_call x14, Pallas kernels, call(): pl.pallas_call(kernel, out_shape=outs, in_specs=specs, out_specs=[VM] * l...  20.9 us
  transfers between devices with their start and end apart: 36, of which 14 were waited for; matrix products, arithmetic and copies ran while one was open for 0% of the time, Pallas kernels for 5%

profile of v1, /device:TPU:0, one launch (start us, length us, event | category | flops | bytes accessed | tf_op | source)
XLA Modules:
  0.0 92.0 jit_solution(17161317006483391009)
XLA Ops:
  0.6 1.5 %shard_map.77 = (f32[8,4,32,128]{3,2,1,0:T(8,128)S(1)}, f32[4,32,128]{2,1,0:T(8,128)S(1)}, s32[4,4,32,128]{3,2,1,0:T(8,128)S(1)}, bf16[60,16,128]{2,1,0:T(8,128)(2,1)S(1)}, bf16[60,16,128]{2,1,0:T(8,128)(2,1)S(1)}) custom-call(f32[8,4,32,128]{3,2,1,0:T(8,128)} %bitcast.10, f32[4,32,128]{2,1,0:T(8,128)} %bitcast.12, s32[4,4,32,128]{3,2,1,0:T(8,128)} %bitcast.11), custom_call_target="tpu_custom_call" | custom-call | tf_op jit(solution)/shard_map/pallas_call | solution.py:680
  2.1 6.4 %collective-permute-start = (bf16[60,16,128]{2,1,0:T(8,128)(2,1)S(1)}, bf16[60,16,128]{2,1,0:T(8,128)(2,1)S(1)}, u32[]{:S(2)}, u32[]{:S(2)}) collective-permute-start(bf16[60,16,128]{2,1,0:T(8,128)(2,1)S(1)} %get-tuple-element.52), channel_id=1, source_target_pairs={{0,15},{1,2},{2,1},{3,4},{4,3},{5,6},{6,5},{7,8},{8,7},{9,10},{10,... | collective-permute-start | bytes 737288 | tf_op jit(solution)/shard_map/ppermute | solution.py:698
  8.5 0.1 shard_map.79
  8.6 2.3 %collective-permute-start.4 = (bf16[30,32,128]{2,1,0:T(8,128)(2,1)S(1)}, bf16[30,32,128]{2,1,0:T(8,128)(2,1)S(1)}, u32[]{:S(2)}, u32[]{:S(2)}) collective-permute-start(bf16[30,32,128]{2,1,0:T(8,128)(2,1)S(1)} %get-tuple-element.58), channel_id=1, source_target_pairs={{0,112},{16,32},{32,16},{48,64},{64,48},{80,96},{96,80},{112,0},{1... | collective-permute-start | bytes 737288 | tf_op jit(solution)/shard_map/ppermute | solution.py:698
  10.9 0.8 collective-permute-start.5
  11.7 2.8 %collective-permute-done.refs_0_.xb = bf16[60,16,128]{2,1,0:T(8,128)(2,1)S(1)} collective-permute-done((bf16[60,16,128]{2,1,0:T(8,128)(2,1)S(1)}, bf16[60,16,128]{2,1,0:T(8,128)(2,1)S(1)}, u32[]{:S(2)}, u32[]{:S(2)}) %collective-permute-start) | collective-permute-done | bytes 245792 | tf_op jit(solution)/shard_map/ppermute | solution.py:698
  14.5 1.5 %collective-permute-done.1.refs_1_.xa = bf16[60,16,128]{2,1,0:T(8,128)(2,1)S(1)} collective-permute-done((bf16[60,16,128]{2,1,0:T(8,128)(2,1)S(1)}, bf16[60,16,128]{2,1,0:T(8,128)(2,1)S(1)}, u32[]{:S(2)}, u32[]{:S(2)}) %collective-permute-start.1) | collective-permute-done | bytes 245792 | tf_op jit(solution)/shard_map/ppermute | solution.py:698
  15.9 0.3 shard_map.78
  16.2 0.1 collective-permute-start.2
  16.3 3.1 %collective-permute-start.3 = (bf16[26,32,128]{2,1,0:T(8,128)(2,1)S(1)}, bf16[26,32,128]{2,1,0:T(8,128)(2,1)S(1)}, u32[]{:S(2)}, u32[]{:S(2)}) collective-permute-start(bf16[26,32,128]{2,1,0:T(8,128)(2,1)S(1)} %get-tuple-element.55), channel_id=1, source_target_pairs={{0,112},{16,32},{32,16},{48,64},{64,48},{80,96},{96,80},{112,0},{1... | collective-permute-start | bytes 638984 | tf_op jit(solution)/shard_map/ppermute | solution.py:698
  19.4 2.8 %shard_map.80 = (f32[4,14,160,128]{3,2,1,0:T(8,128)S(1)}, f32[4,14,160,128]{3,2,1,0:T(8,128)S(1)}, f32[14,160,128]{2,1,0:T(8,128)S(1)}, f32[4,14,160,128]{3,2,1,...) custom-call(bf16[60,16,128]{2,1,0:T(8,128)(2,1)S(1)} %collective-permute-done.refs_0_.xb, ...), custom_call_target="tpu_custom_call" | custom-call | flops 4194304 | bytes 4194304 | tf_op jit(solution)/shard_map/pallas_call | solution.py:680
  22.2 0.7 collective-permute-done.3.cb
  23.0 5.0 %shard_map.81 = (f32[8,4,32,128]{3,2,1,0:T(8,128)S(1)}, f32[96,128]{1,0:T(8,128)S(1)}, bf16[96,128]{1,0:T(8,128)(2,1)S(1)}, bf16[32,128]{1,0:T(8,128)(2,1)S(1)},...) custom-call(s32[8]{0:T(128)} %plan_far.7, ...), custom_call_target="tpu_custom_call", output_to_operand_aliasing={{4}: (4, {}), {5}: (5, {}), {6}: (6, {}), {7}: (7, {}), {8}... | custom-call | tf_op jit(solution)/shard_map/pallas_call | solution.py:680
  27.9 4.0 %collective-permute-start.11 = (bf16[32,128]{1,0:T(8,128)(2,1)S(1)}, bf16[32,128]{1,0:T(8,128)(2,1)S(1)}, u32[]{:S(2)}, u32[]{:S(2)}) collective-permute-start(bf16[32,128]{1,0:T(8,128)(2,1)S(1)} %get-tuple-element.73), channel_id=1, source_target_pairs={{0,15},{1,2},{2,1},{3,4},{4,3},{5,6},{6,5},{7,8},{8,7},{9,10},{10,... | collective-permute-start | bytes 24584 | tf_op jit(solution)/shard_map/ppermute | solution.py:698
  32.0 2.4 %collective-permute-start.9 = (bf16[32,128]{1,0:T(8,128)(2,1)S(1)}, bf16[32,128]{1,0:T(8,128)(2,1)S(1)}, u32[]{:S(2)}, u32[]{:S(2)}) collective-permute-start(bf16[32,128]{1,0:T(8,128)(2,1)S(1)} %get-tuple-element.73), channel_id=1, source_target_pairs={{0,112},{16,32},{32,16},{48,64},{64,48},{80,96},{96,80},{112,0},{1... | collective-permute-start | bytes 24584 | tf_op jit(solution)/shard_map/ppermute | solution.py:698
  34.4 0.6 collective-permute-done.11.xb
  35.0 0.6 collective-permute-done.10.xa
  35.6 0.6 collective-permute-done.9.tb
  36.2 0.5 shard_map.82
  36.7 2.8 %collective-permute-start.15 = (bf16[32,128]{1,0:T(8,128)(2,1)S(1)}, bf16[32,128]{1,0:T(8,128)(2,1)S(1)}, u32[]{:S(2)}, u32[]{:S(2)}) collective-permute-start(bf16[32,128]{1,0:T(8,128)(2,1)S(1)} %get-tuple-element.76), channel_id=1, source_target_pairs={{0,15},{1,2},{2,1},{3,4},{4,3},{5,6},{6,5},{7,8},{8,7},{9,10},{10,... | collective-permute-start | bytes 24584 | tf_op jit(solution)/shard_map/ppermute | solution.py:698
  39.5 1.3 %collective-permute-start.13 = (bf16[32,128]{1,0:T(8,128)(2,1)S(1)}, bf16[32,128]{1,0:T(8,128)(2,1)S(1)}, u32[]{:S(2)}, u32[]{:S(2)}) collective-permute-start(bf16[32,128]{1,0:T(8,128)(2,1)S(1)} %get-tuple-element.76), channel_id=1, source_target_pairs={{0,112},{16,32},{32,16},{48,64},{64,48},{80,96},{96,80},{112,0},{1... | collective-permute-start | bytes 24584 | tf_op jit(solution)/shard_map/ppermute | solution.py:698
  40.8 3.0 %collective-permute-done.15.xb = bf16[32,128]{1,0:T(8,128)(2,1)S(1)} collective-permute-done((bf16[32,128]{1,0:T(8,128)(2,1)S(1)}, bf16[32,128]{1,0:T(8,128)(2,1)S(1)}, u32[]{:S(2)}, u32[]{:S(2)}) %collective-permute-start.15) | collective-permute-done | bytes 8224 | tf_op jit(solution)/shard_map/ppermute | solution.py:698
  43.8 0.5 shard_map.83
  44.2 2.8 %collective-permute-start.19 = (bf16[32,128]{1,0:T(8,128)(2,1)S(1)}, bf16[32,128]{1,0:T(8,128)(2,1)S(1)}, u32[]{:S(2)}, u32[]{:S(2)}) collective-permute-start(bf16[32,128]{1,0:T(8,128)(2,1)S(1)} %get-tuple-element.79), channel_id=1, source_target_pairs={{0,15},{1,2},{2,1},{3,4},{4,3},{5,6},{6,5},{7,8},{8,7},{9,10},{10,... | collective-permute-start | bytes 24584 | tf_op jit(solution)/shard_map/ppermute | solution.py:698
  47.0 1.8 %collective-permute-start.17 = (bf16[32,128]{1,0:T(8,128)(2,1)S(1)}, bf16[32,128]{1,0:T(8,128)(2,1)S(1)}, u32[]{:S(2)}, u32[]{:S(2)}) collective-permute-start(bf16[32,128]{1,0:T(8,128)(2,1)S(1)} %get-tuple-element.79), channel_id=1, source_target_pairs={{0,112},{16,32},{32,16},{48,64},{64,48},{80,96},{96,80},{112,0},{1... | collective-permute-start | bytes 24584 | tf_op jit(solution)/shard_map/ppermute | solution.py:698
  48.8 2.4 %collective-permute-done.19.xb = bf16[32,128]{1,0:T(8,128)(2,1)S(1)} collective-permute-done((bf16[32,128]{1,0:T(8,128)(2,1)S(1)}, bf16[32,128]{1,0:T(8,128)(2,1)S(1)}, u32[]{:S(2)}, u32[]{:S(2)}) %collective-permute-start.19) | collective-permute-done | bytes 8224 | tf_op jit(solution)/shard_map/ppermute | solution.py:698
  51.3 0.5 shard_map.84
  51.8 2.8 %collective-permute-start.23 = (bf16[32,128]{1,0:T(8,128)(2,1)S(1)}, bf16[32,128]{1,0:T(8,128)(2,1)S(1)}, u32[]{:S(2)}, u32[]{:S(2)}) collective-permute-start(bf16[32,128]{1,0:T(8,128)(2,1)S(1)} %get-tuple-element.82), channel_id=1, source_target_pairs={{0,15},{1,2},{2,1},{3,4},{4,3},{5,6},{6,5},{7,8},{8,7},{9,10},{10,... | collective-permute-start | bytes 24584 | tf_op jit(solution)/shard_map/ppermute | solution.py:698
  54.5 1.0 %collective-permute-start.21 = (bf16[32,128]{1,0:T(8,128)(2,1)S(1)}, bf16[32,128]{1,0:T(8,128)(2,1)S(1)}, u32[]{:S(2)}, u32[]{:S(2)}) collective-permute-start(bf16[32,128]{1,0:T(8,128)(2,1)S(1)} %get-tuple-element.82), channel_id=1, source_target_pairs={{0,112},{16,32},{32,16},{48,64},{64,48},{80,96},{96,80},{112,0},{1... | collective-permute-start | bytes 24584 | tf_op jit(solution)/shard_map/ppermute | solution.py:698
  55.5 3.3 %collective-permute-done.23.xb = bf16[32,128]{1,0:T(8,128)(2,1)S(1)} collective-permute-done((bf16[32,128]{1,0:T(8,128)(2,1)S(1)}, bf16[32,128]{1,0:T(8,128)(2,1)S(1)}, u32[]{:S(2)}, u32[]{:S(2)}) %collective-permute-start.23) | collective-permute-done | bytes 8224 | tf_op jit(solution)/shard_map/ppermute | solution.py:698
  58.8 0.5 shard_map.85
  59.3 2.8 %collective-permute-start.27 = (bf16[32,128]{1,0:T(8,128)(2,1)S(1)}, bf16[32,128]{1,0:T(8,128)(2,1)S(1)}, u32[]{:S(2)}, u32[]{:S(2)}) collective-permute-start(bf16[32,128]{1,0:T(8,128)(2,1)S(1)} %get-tuple-element.85), channel_id=1, source_target_pairs={{0,15},{1,2},{2,1},{3,4},{4,3},{5,6},{6,5},{7,8},{8,7},{9,10},{10,... | collective-permute-start | bytes 24584 | tf_op jit(solution)/shard_map/ppermute | solution.py:698
  62.0 1.2 %collective-permute-start.25 = (bf16[32,128]{1,0:T(8,128)(2,1)S(1)}, bf16[32,128]{1,0:T(8,128)(2,1)S(1)}, u32[]{:S(2)}, u32[]{:S(2)}) collective-permute-start(bf16[32,128]{1,0:T(8,128)(2,1)S(1)} %get-tuple-element.85), channel_id=1, source_target_pairs={{0,112},{16,32},{32,16},{48,64},{64,48},{80,96},{96,80},{112,0},{1... | collective-permute-start | bytes 24584 | tf_op jit(solution)/shard_map/ppermute | solution.py:698
  63.3 3.0 %collective-permute-done.27.xb = bf16[32,128]{1,0:T(8,128)(2,1)S(1)} collective-permute-done((bf16[32,128]{1,0:T(8,128)(2,1)S(1)}, bf16[32,128]{1,0:T(8,128)(2,1)S(1)}, u32[]{:S(2)}, u32[]{:S(2)}) %collective-permute-start.27) | collective-permute-done | bytes 8224 | tf_op jit(solution)/shard_map/ppermute | solution.py:698
  66.3 2.1 %shard_map.86 = (f32[8,4,32,128]{3,2,1,0:T(8,128)S(1)}, bf16[48,16,128]{2,1,0:T(8,128)(2,1)S(1)}, bf16[48,16,128]{2,1,0:T(8,128)(2,1)S(1)}) custom-call(f32[7,6,48,128]{3,2,1,0:T(8,128)S(1)} %get-tuple-element.70.operator, f32[96,128]{1,0:T(8,128)S(1)} %get-tuple-element.71.rhs.estimate, f32[96,128]{1,0:T(8,128)S(1)} %get-tuple-element.83.estimate, ...), custom_call_target="tpu_custom_call" | custom-call | tf_op jit(solution)/shard_map/pallas_call | solution.py:680
  68.5 0.1 shard_map.87
  68.6 1.3 %collective-permute-start.30 = (bf16[20,32,128]{2,1,0:T(8,128)(2,1)S(1)}, bf16[20,32,128]{2,1,0:T(8,128)(2,1)S(1)}, u32[]{:S(2)}, u32[]{:S(2)}) collective-permute-start(bf16[20,32,128]{2,1,0:T(8,128)(2,1)S(1)} %get-tuple-element.90), channel_id=1, source_target_pairs={{0,112},{16,32},{32,16},{48,64},{64,48},{80,96},{96,80},{112,0},{1... | collective-permute-start | bytes 491528 | tf_op jit(solution)/shard_map/ppermute | solution.py:698
  69.9 2.4 %collective-permute-start.28 = (bf16[48,16,128]{2,1,0:T(8,128)(2,1)S(1)}, bf16[48,16,128]{2,1,0:T(8,128)(2,1)S(1)}, u32[]{:S(2)}, u32[]{:S(2)}) collective-permute-start(bf16[48,16,128]{2,1,0:T(8,128)(2,1)S(1)} %get-tuple-element.87), channel_id=1, source_target_pairs={{0,15},{1,2},{2,1},{3,4},{4,3},{5,6},{6,5},{7,8},{8,7},{9,10},{10,... | collective-permute-start | bytes 589832 | tf_op jit(solution)/shard_map/ppermute | solution.py:698
  72.3 1.7 %collective-permute-start.31 = (bf16[20,32,128]{2,1,0:T(8,128)(2,1)S(1)}, bf16[20,32,128]{2,1,0:T(8,128)(2,1)S(1)}, u32[]{:S(2)}, u32[]{:S(2)}) collective-permute-start(bf16[20,32,128]{2,1,0:T(8,128)(2,1)S(1)} %get-tuple-element.91), channel_id=1, source_target_pairs={{0,112},{16,32},{32,16},{48,64},{64,48},{80,96},{96,80},{112,0},{1... | collective-permute-start | bytes 491528 | tf_op jit(solution)/shard_map/ppermute | solution.py:698
  74.0 0.6 collective-permute-done.30.tb2.refs_5_
  74.6 3.7 %collective-permute-done.31.tb1.refs_4_ = bf16[20,32,128]{2,1,0:T(8,128)(2,1)S(1)} collective-permute-done((bf16[20,32,128]{2,1,0:T(8,128)(2,1)S(1)}, bf16[20,32,128]{2,1,0:T(8,128)(2,1)S(1)}, u32[]{:S(2)}, u32[]{:S(2)}) %collective-permute-start.31) | collective-permute-done | bytes 163872 | tf_op jit(solution)/shard_map/ppermute | solution.py:698
  78.3 0.6 collective-permute-done.28.xb.refs_0_
  78.9 0.2 shard_map.89
  79.1 0.1 collective-permute-start.34
  79.2 2.0 %collective-permute-start.35 = (bf16[32,32,128]{2,1,0:T(8,128)(2,1)S(1)}, bf16[32,32,128]{2,1,0:T(8,128)(2,1)S(1)}, u32[]{:S(2)}, u32[]{:S(2)}) collective-permute-start(bf16[32,32,128]{2,1,0:T(8,128)(2,1)S(1)} %get-tuple-element.97), channel_id=1, source_target_pairs={{0,112},{16,32},{32,16},{48,64},{64,48},{80,96},{96,80},{112,0},{1... | collective-permute-start | bytes 786440 | tf_op jit(solution)/shard_map/ppermute | solution.py:698
  81.3 1.5 %shard_map.88 = (f32[4,14,160,128]{3,2,1,0:T(8,128)S(1)}, f32[4,14,160,128]{3,2,1,0:T(8,128)S(1)}) custom-call(bf16[48,16,128]{2,1,0:T(8,128)(2,1)S(1)} %collective-permute-done.28.xb.refs_0_, bf16[48,16,128]{2,1,0:T(8,128)(2,1)S(1)} %collective-permute-done.29.xa.refs_1_, bf16[20,32,128]{2,1,0:T(8,128)(2,1)S(1)} %collective-permute-done.30.tb2.refs_5_, ...), custom_call_target="tpu_custom_call" | custom-call | flops 4194304 | bytes 4194304 | tf_op jit(solution)/shard_map/pallas_call | solution.py:680
  82.7 3.6 %collective-permute-done.35.cb = bf16[32,32,128]{2,1,0:T(8,128)(2,1)S(1)} collective-permute-done((bf16[32,32,128]{2,1,0:T(8,128)(2,1)S(1)}, bf16[32,32,128]{2,1,0:T(8,128)(2,1)S(1)}, u32[]{:S(2)}, u32[]{:S(2)}) %collective-permute-start.35) | collective-permute-done | bytes 262176 | tf_op jit(solution)/shard_map/ppermute | solution.py:698
  86.3 5.5 %shard_map.90 = (f32[8,4,32,128]{3,2,1,0:T(8,128)}, f32[8,4,32,128]{3,2,1,0:T(8,128)}, f32[4,14,160,128]{3,2,1,0:T(8,128)S(1)}, f32[4,14,160,128]{3,2,1,0:T(8,128)S(1)}) custom-call(s32[8]{0:T(128)} %plan_far.7, f32[4,32,128]{2,1,0:T(8,128)S(1)} %get-tuple-element.51.mass, ...), custom_call_target="tpu_custom_call", output_to_operand_aliasing={{2}: (5, {}), {3}: (6, {})} | custom-call | tf_op jit(solution)/shard_map/pallas_call | solution.py:680
  (40 shorter events, 0.1 us)
Async XLA Ops:
  0.6 22.3 %copy-start = (bf16[24,4,4,8,4,128]{5,4,3,2,1,0:T(4,128)(2,1)S(1)}, bf16[24,4,4,8,4,128]{5,4,3,2,1,0:T(4,128)(2,1)}, u32[]{:S(2)}) copy-start(bf16[24,4,4,8,4,128]{5,4,3,2,1,0:T(4,128)(2,1)} %param.9) | copy-start | bytes 9437188
  2.1 12.3 %collective-permute-start = (bf16[60,16,128]{2,1,0:T(8,128)(2,1)S(1)}, bf16[60,16,128]{2,1,0:T(8,128)(2,1)S(1)}, u32[]{:S(2)}, u32[]{:S(2)}) collective-permute-start(bf16[60,16,128]{2,1,0:T(8,128)(2,1)S(1)} %get-tuple-element.52), channel_id=1, source_target_pairs={{0,15},{1,2},{2,1},{3,4},{4,3},{5,6},{6,5},{7,8},{8,7},{9,10},{10,... | collective-permute-start | bytes 737288 | tf_op jit(solution)/shard_map/ppermute | solution.py:698
  8.5 7.4 %collective-permute-start.1 = (bf16[60,16,128]{2,1,0:T(8,128)(2,1)S(1)}, bf16[60,16,128]{2,1,0:T(8,128)(2,1)S(1)}, u32[]{:S(2)}, u32[]{:S(2)}) collective-permute-start(bf16[60,16,128]{2,1,0:T(8,128)(2,1)S(1)} %get-tuple-element.53), channel_id=1, source_target_pairs={{0,1},{1,0},{2,3},{3,2},{4,5},{5,4},{6,7},{7,6},{8,9},{9,8},{10,11... | collective-permute-start | bytes 737288 | tf_op jit(solution)/shard_map/ppermute | solution.py:698
  8.6 7.7 %collective-permute-start.4 = (bf16[30,32,128]{2,1,0:T(8,128)(2,1)S(1)}, bf16[30,32,128]{2,1,0:T(8,128)(2,1)S(1)}, u32[]{:S(2)}, u32[]{:S(2)}) collective-permute-start(bf16[30,32,128]{2,1,0:T(8,128)(2,1)S(1)} %get-tuple-element.58), channel_id=1, source_target_pairs={{0,112},{16,32},{32,16},{48,64},{64,48},{80,96},{96,80},{112,0},{1... | collective-permute-start | bytes 737288 | tf_op jit(solution)/shard_map/ppermute | solution.py:698
  10.9 8.5 %collective-permute-start.5 = (bf16[30,32,128]{2,1,0:T(8,128)(2,1)S(1)}, bf16[30,32,128]{2,1,0:T(8,128)(2,1)S(1)}, u32[]{:S(2)}, u32[]{:S(2)}) collective-permute-start(bf16[30,32,128]{2,1,0:T(8,128)(2,1)S(1)} %get-tuple-element.59), channel_id=1, source_target_pairs={{0,112},{16,32},{32,16},{48,64},{64,48},{80,96},{96,80},{112,0},{1... | collective-permute-start | bytes 737288 | tf_op jit(solution)/shard_map/ppermute | solution.py:698
  11.7 7.8 %collective-permute-start.6 = (bf16[30,32,128]{2,1,0:T(8,128)(2,1)S(1)}, bf16[30,32,128]{2,1,0:T(8,128)(2,1)S(1)}, u32[]{:S(2)}, u32[]{:S(2)}) collective-permute-start(bf16[30,32,128]{2,1,0:T(8,128)(2,1)S(1)} %get-tuple-element.60), channel_id=1, source_target_pairs={{0,16},{16,0},{32,48},{48,32},{64,80},{80,64},{96,112},{112,96},{1... | collective-permute-start | bytes 737288 | tf_op jit(solution)/shard_map/ppermute | solution.py:698
  14.5 5.0 %collective-permute-start.7 = (bf16[30,32,128]{2,1,0:T(8,128)(2,1)S(1)}, bf16[30,32,128]{2,1,0:T(8,128)(2,1)S(1)}, u32[]{:S(2)}, u32[]{:S(2)}) collective-permute-start(bf16[30,32,128]{2,1,0:T(8,128)(2,1)S(1)} %get-tuple-element.61), channel_id=1, source_target_pairs={{0,16},{16,0},{32,48},{48,32},{64,80},{80,64},{96,112},{112,96},{1... | collective-permute-start | bytes 737288 | tf_op jit(solution)/shard_map/ppermute | solution.py:698
  16.2 6.0 %collective-permute-start.2 = (bf16[26,32,128]{2,1,0:T(8,128)(2,1)S(1)}, bf16[26,32,128]{2,1,0:T(8,128)(2,1)S(1)}, u32[]{:S(2)}, u32[]{:S(2)}) collective-permute-start(bf16[26,32,128]{2,1,0:T(8,128)(2,1)S(1)} %get-tuple-element.54), channel_id=1, source_target_pairs={{0,16},{16,0},{32,48},{48,32},{64,80},{80,64},{96,112},{112,96},{1... | collective-permute-start | bytes 638984 | tf_op jit(solution)/shard_map/ppermute | solution.py:698
  16.3 6.6 %collective-permute-start.3 = (bf16[26,32,128]{2,1,0:T(8,128)(2,1)S(1)}, bf16[26,32,128]{2,1,0:T(8,128)(2,1)S(1)}, u32[]{:S(2)}, u32[]{:S(2)}) collective-permute-start(bf16[26,32,128]{2,1,0:T(8,128)(2,1)S(1)} %get-tuple-element.55), channel_id=1, source_target_pairs={{0,112},{16,32},{32,16},{48,64},{64,48},{80,96},{96,80},{112,0},{1... | collective-permute-start | bytes 638984 | tf_op jit(solution)/shard_map/ppermute | solution.py:698
  27.9 7.1 %collective-permute-start.11 = (bf16[32,128]{1,0:T(8,128)(2,1)S(1)}, bf16[32,128]{1,0:T(8,128)(2,1)S(1)}, u32[]{:S(2)}, u32[]{:S(2)}) collective-permute-start(bf16[32,128]{1,0:T(8,128)(2,1)S(1)} %get-tuple-element.73), channel_id=1, source_target_pairs={{0,15},{1,2},{2,1},{3,4},{4,3},{5,6},{6,5},{7,8},{8,7},{9,10},{10,... | collective-permute-start | bytes 24584 | tf_op jit(solution)/shard_map/ppermute | solution.py:698
  32.0 3.7 %collective-permute-start.10 = (bf16[32,128]{1,0:T(8,128)(2,1)S(1)}, bf16[32,128]{1,0:T(8,128)(2,1)S(1)}, u32[]{:S(2)}, u32[]{:S(2)}) collective-permute-start(bf16[32,128]{1,0:T(8,128)(2,1)S(1)} %get-tuple-element.73), channel_id=1, source_target_pairs={{0,1},{1,0},{2,3},{3,2},{4,5},{5,4},{6,7},{7,6},{8,9},{9,8},{10,11... | collective-permute-start | bytes 24584 | tf_op jit(solution)/shard_map/ppermute | solution.py:698
  32.0 4.3 %collective-permute-start.9 = (bf16[32,128]{1,0:T(8,128)(2,1)S(1)}, bf16[32,128]{1,0:T(8,128)(2,1)S(1)}, u32[]{:S(2)}, u32[]{:S(2)}) collective-permute-start(bf16[32,128]{1,0:T(8,128)(2,1)S(1)} %get-tuple-element.73), channel_id=1, source_target_pairs={{0,112},{16,32},{32,16},{48,64},{64,48},{80,96},{96,80},{112,0},{1... | collective-permute-start | bytes 24584 | tf_op jit(solution)/shard_map/ppermute | solution.py:698
  34.4 1.9 %collective-permute-start.8 = (bf16[32,128]{1,0:T(8,128)(2,1)S(1)}, bf16[32,128]{1,0:T(8,128)(2,1)S(1)}, u32[]{:S(2)}, u32[]{:S(2)}) collective-permute-start(bf16[32,128]{1,0:T(8,128)(2,1)S(1)} %get-tuple-element.73), channel_id=1, source_target_pairs={{0,16},{16,0},{32,48},{48,32},{64,80},{80,64},{96,112},{112,96},{1... | collective-permute-start | bytes 24584 | tf_op jit(solution)/shard_map/ppermute | solution.py:698
  36.7 7.1 %collective-permute-start.15 = (bf16[32,128]{1,0:T(8,128)(2,1)S(1)}, bf16[32,128]{1,0:T(8,128)(2,1)S(1)}, u32[]{:S(2)}, u32[]{:S(2)}) collective-permute-start(bf16[32,128]{1,0:T(8,128)(2,1)S(1)} %get-tuple-element.76), channel_id=1, source_target_pairs={{0,15},{1,2},{2,1},{3,4},{4,3},{5,6},{6,5},{7,8},{8,7},{9,10},{10,... | collective-permute-start | bytes 24584 | tf_op jit(solution)/shard_map/ppermute | solution.py:698
  39.5 4.3 %collective-permute-start.14 = (bf16[32,128]{1,0:T(8,128)(2,1)S(1)}, bf16[32,128]{1,0:T(8,128)(2,1)S(1)}, u32[]{:S(2)}, u32[]{:S(2)}) collective-permute-start(bf16[32,128]{1,0:T(8,128)(2,1)S(1)} %get-tuple-element.76), channel_id=1, source_target_pairs={{0,1},{1,0},{2,3},{3,2},{4,5},{5,4},{6,7},{7,6},{8,9},{9,8},{10,11... | collective-permute-start | bytes 24584 | tf_op jit(solution)/shard_map/ppermute | solution.py:698
  39.5 4.3 %collective-permute-start.13 = (bf16[32,128]{1,0:T(8,128)(2,1)S(1)}, bf16[32,128]{1,0:T(8,128)(2,1)S(1)}, u32[]{:S(2)}, u32[]{:S(2)}) collective-permute-start(bf16[32,128]{1,0:T(8,128)(2,1)S(1)} %get-tuple-element.76), channel_id=1, source_target_pairs={{0,112},{16,32},{32,16},{48,64},{64,48},{80,96},{96,80},{112,0},{1... | collective-permute-start | bytes 24584 | tf_op jit(solution)/shard_map/ppermute | solution.py:698
  40.8 3.0 %collective-permute-start.12 = (bf16[32,128]{1,0:T(8,128)(2,1)S(1)}, bf16[32,128]{1,0:T(8,128)(2,1)S(1)}, u32[]{:S(2)}, u32[]{:S(2)}) collective-permute-start(bf16[32,128]{1,0:T(8,128)(2,1)S(1)} %get-tuple-element.76), channel_id=1, source_target_pairs={{0,16},{16,0},{32,48},{48,32},{64,80},{80,64},{96,112},{112,96},{1... | collective-permute-start | bytes 24584 | tf_op jit(solution)/shard_map/ppermute | solution.py:698
  44.2 7.1 %collective-permute-start.19 = (bf16[32,128]{1,0:T(8,128)(2,1)S(1)}, bf16[32,128]{1,0:T(8,128)(2,1)S(1)}, u32[]{:S(2)}, u32[]{:S(2)}) collective-permute-start(bf16[32,128]{1,0:T(8,128)(2,1)S(1)} %get-tuple-element.79), channel_id=1, source_target_pairs={{0,15},{1,2},{2,1},{3,4},{4,3},{5,6},{6,5},{7,8},{8,7},{9,10},{10,... | collective-permute-start | bytes 24584 | tf_op jit(solution)/shard_map/ppermute | solution.py:698
  47.0 4.3 %collective-permute-start.18 = (bf16[32,128]{1,0:T(8,128)(2,1)S(1)}, bf16[32,128]{1,0:T(8,128)(2,1)S(1)}, u32[]{:S(2)}, u32[]{:S(2)}) collective-permute-start(bf16[32,128]{1,0:T(8,128)(2,1)S(1)} %get-tuple-element.79), channel_id=1, source_target_pairs={{0,1},{1,0},{2,3},{3,2},{4,5},{5,4},{6,7},{7,6},{8,9},{9,8},{10,11... | collective-permute-start | bytes 24584 | tf_op jit(solution)/shard_map/ppermute | solution.py:698
  47.0 4.3 %collective-permute-start.17 = (bf16[32,128]{1,0:T(8,128)(2,1)S(1)}, bf16[32,128]{1,0:T(8,128)(2,1)S(1)}, u32[]{:S(2)}, u32[]{:S(2)}) collective-permute-start(bf16[32,128]{1,0:T(8,128)(2,1)S(1)} %get-tuple-element.79), channel_id=1, source_target_pairs={{0,112},{16,32},{32,16},{48,64},{64,48},{80,96},{96,80},{112,0},{1... | collective-permute-start | bytes 24584 | tf_op jit(solution)/shard_map/ppermute | solution.py:698
  48.8 2.4 %collective-permute-start.16 = (bf16[32,128]{1,0:T(8,128)(2,1)S(1)}, bf16[32,128]{1,0:T(8,128)(2,1)S(1)}, u32[]{:S(2)}, u32[]{:S(2)}) collective-permute-start(bf16[32,128]{1,0:T(8,128)(2,1)S(1)} %get-tuple-element.79), channel_id=1, source_target_pairs={{0,16},{16,0},{32,48},{48,32},{64,80},{80,64},{96,112},{112,96},{1... | collective-permute-start | bytes 24584 | tf_op jit(solution)/shard_map/ppermute | solution.py:698
  51.8 7.1 %collective-permute-start.23 = (bf16[32,128]{1,0:T(8,128)(2,1)S(1)}, bf16[32,128]{1,0:T(8,128)(2,1)S(1)}, u32[]{:S(2)}, u32[]{:S(2)}) collective-permute-start(bf16[32,128]{1,0:T(8,128)(2,1)S(1)} %get-tuple-element.82), channel_id=1, source_target_pairs={{0,15},{1,2},{2,1},{3,4},{4,3},{5,6},{6,5},{7,8},{8,7},{9,10},{10,... | collective-permute-start | bytes 24584 | tf_op jit(solution)/shard_map/ppermute | solution.py:698
  54.5 4.3 %collective-permute-start.22 = (bf16[32,128]{1,0:T(8,128)(2,1)S(1)}, bf16[32,128]{1,0:T(8,128)(2,1)S(1)}, u32[]{:S(2)}, u32[]{:S(2)}) collective-permute-start(bf16[32,128]{1,0:T(8,128)(2,1)S(1)} %get-tuple-element.82), channel_id=1, source_target_pairs={{0,1},{1,0},{2,3},{3,2},{4,5},{5,4},{6,7},{7,6},{8,9},{9,8},{10,11... | collective-permute-start | bytes 24584 | tf_op jit(solution)/shard_map/ppermute | solution.py:698
  54.5 4.3 %collective-permute-start.21 = (bf16[32,128]{1,0:T(8,128)(2,1)S(1)}, bf16[32,128]{1,0:T(8,128)(2,1)S(1)}, u32[]{:S(2)}, u32[]{:S(2)}) collective-permute-start(bf16[32,128]{1,0:T(8,128)(2,1)S(1)} %get-tuple-element.82), channel_id=1, source_target_pairs={{0,112},{16,32},{32,16},{48,64},{64,48},{80,96},{96,80},{112,0},{1... | collective-permute-start | bytes 24584 | tf_op jit(solution)/shard_map/ppermute | solution.py:698
  55.5 3.3 %collective-permute-start.20 = (bf16[32,128]{1,0:T(8,128)(2,1)S(1)}, bf16[32,128]{1,0:T(8,128)(2,1)S(1)}, u32[]{:S(2)}, u32[]{:S(2)}) collective-permute-start(bf16[32,128]{1,0:T(8,128)(2,1)S(1)} %get-tuple-element.82), channel_id=1, source_target_pairs={{0,16},{16,0},{32,48},{48,32},{64,80},{80,64},{96,112},{112,96},{1... | collective-permute-start | bytes 24584 | tf_op jit(solution)/shard_map/ppermute | solution.py:698
  59.3 7.1 %collective-permute-start.27 = (bf16[32,128]{1,0:T(8,128)(2,1)S(1)}, bf16[32,128]{1,0:T(8,128)(2,1)S(1)}, u32[]{:S(2)}, u32[]{:S(2)}) collective-permute-start(bf16[32,128]{1,0:T(8,128)(2,1)S(1)} %get-tuple-element.85), channel_id=1, source_target_pairs={{0,15},{1,2},{2,1},{3,4},{4,3},{5,6},{6,5},{7,8},{8,7},{9,10},{10,... | collective-permute-start | bytes 24584 | tf_op jit(solution)/shard_map/ppermute | solution.py:698
  62.0 4.3 %collective-permute-start.26 = (bf16[32,128]{1,0:T(8,128)(2,1)S(1)}, bf16[32,128]{1,0:T(8,128)(2,1)S(1)}, u32[]{:S(2)}, u32[]{:S(2)}) collective-permute-start(bf16[32,128]{1,0:T(8,128)(2,1)S(1)} %get-tuple-element.85), channel_id=1, source_target_pairs={{0,1},{1,0},{2,3},{3,2},{4,5},{5,4},{6,7},{7,6},{8,9},{9,8},{10,11... | collective-permute-start | bytes 24584 | tf_op jit(solution)/shard_map/ppermute | solution.py:698
  62.0 4.3 %collective-permute-start.25 = (bf16[32,128]{1,0:T(8,128)(2,1)S(1)}, bf16[32,128]{1,0:T(8,128)(2,1)S(1)}, u32[]{:S(2)}, u32[]{:S(2)}) collective-permute-start(bf16[32,128]{1,0:T(8,128)(2,1)S(1)} %get-tuple-element.85), channel_id=1, source_target_pairs={{0,112},{16,32},{32,16},{48,64},{64,48},{80,96},{96,80},{112,0},{1... | collective-permute-start | bytes 24584 | tf_op jit(solution)/shard_map/ppermute | solution.py:698
  63.3 3.0 %collective-permute-start.24 = (bf16[32,128]{1,0:T(8,128)(2,1)S(1)}, bf16[32,128]{1,0:T(8,128)(2,1)S(1)}, u32[]{:S(2)}, u32[]{:S(2)}) collective-permute-start(bf16[32,128]{1,0:T(8,128)(2,1)S(1)} %get-tuple-element.85), channel_id=1, source_target_pairs={{0,16},{16,0},{32,48},{48,32},{64,80},{80,64},{96,112},{112,96},{1... | collective-permute-start | bytes 24584 | tf_op jit(solution)/shard_map/ppermute | solution.py:698
  68.6 6.0 %collective-permute-start.30 = (bf16[20,32,128]{2,1,0:T(8,128)(2,1)S(1)}, bf16[20,32,128]{2,1,0:T(8,128)(2,1)S(1)}, u32[]{:S(2)}, u32[]{:S(2)}) collective-permute-start(bf16[20,32,128]{2,1,0:T(8,128)(2,1)S(1)} %get-tuple-element.90), channel_id=1, source_target_pairs={{0,112},{16,32},{32,16},{48,64},{64,48},{80,96},{96,80},{112,0},{1... | collective-permute-start | bytes 491528 | tf_op jit(solution)/shard_map/ppermute | solution.py:698
  69.9 9.0 %collective-permute-start.28 = (bf16[48,16,128]{2,1,0:T(8,128)(2,1)S(1)}, bf16[48,16,128]{2,1,0:T(8,128)(2,1)S(1)}, u32[]{:S(2)}, u32[]{:S(2)}) collective-permute-start(bf16[48,16,128]{2,1,0:T(8,128)(2,1)S(1)} %get-tuple-element.87), channel_id=1, source_target_pairs={{0,15},{1,2},{2,1},{3,4},{4,3},{5,6},{6,5},{7,8},{8,7},{9,10},{10,... | collective-permute-start | bytes 589832 | tf_op jit(solution)/shard_map/ppermute | solution.py:698
  72.3 6.6 %collective-permute-start.29 = (bf16[48,16,128]{2,1,0:T(8,128)(2,1)S(1)}, bf16[48,16,128]{2,1,0:T(8,128)(2,1)S(1)}, u32[]{:S(2)}, u32[]{:S(2)}) collective-permute-start(bf16[48,16,128]{2,1,0:T(8,128)(2,1)S(1)} %get-tuple-element.88), channel_id=1, source_target_pairs={{0,1},{1,0},{2,3},{3,2},{4,5},{5,4},{6,7},{7,6},{8,9},{9,8},{10,11... | collective-permute-start | bytes 589832 | tf_op jit(solution)/shard_map/ppermute | solution.py:698
  72.3 6.0 %collective-permute-start.31 = (bf16[20,32,128]{2,1,0:T(8,128)(2,1)S(1)}, bf16[20,32,128]{2,1,0:T(8,128)(2,1)S(1)}, u32[]{:S(2)}, u32[]{:S(2)}) collective-permute-start(bf16[20,32,128]{2,1,0:T(8,128)(2,1)S(1)} %get-tuple-element.91), channel_id=1, source_target_pairs={{0,112},{16,32},{32,16},{48,64},{64,48},{80,96},{96,80},{112,0},{1... | collective-permute-start | bytes 491528 | tf_op jit(solution)/shard_map/ppermute | solution.py:698
  74.0 4.3 %collective-permute-start.32 = (bf16[20,32,128]{2,1,0:T(8,128)(2,1)S(1)}, bf16[20,32,128]{2,1,0:T(8,128)(2,1)S(1)}, u32[]{:S(2)}, u32[]{:S(2)}) collective-permute-start(bf16[20,32,128]{2,1,0:T(8,128)(2,1)S(1)} %get-tuple-element.92), channel_id=1, source_target_pairs={{0,16},{16,0},{32,48},{48,32},{64,80},{80,64},{96,112},{112,96},{1... | collective-permute-start | bytes 491528 | tf_op jit(solution)/shard_map/ppermute | solution.py:698
  74.6 3.7 %collective-permute-start.33 = (bf16[20,32,128]{2,1,0:T(8,128)(2,1)S(1)}, bf16[20,32,128]{2,1,0:T(8,128)(2,1)S(1)}, u32[]{:S(2)}, u32[]{:S(2)}) collective-permute-start(bf16[20,32,128]{2,1,0:T(8,128)(2,1)S(1)} %get-tuple-element.93), channel_id=1, source_target_pairs={{0,16},{16,0},{32,48},{48,32},{64,80},{80,64},{96,112},{112,96},{1... | collective-permute-start | bytes 491528 | tf_op jit(solution)/shard_map/ppermute | solution.py:698
  79.1 3.6 %collective-permute-start.34 = (bf16[32,32,128]{2,1,0:T(8,128)(2,1)S(1)}, bf16[32,32,128]{2,1,0:T(8,128)(2,1)S(1)}, u32[]{:S(2)}, u32[]{:S(2)}) collective-permute-start(bf16[32,32,128]{2,1,0:T(8,128)(2,1)S(1)} %get-tuple-element.96), channel_id=1, source_target_pairs={{0,16},{16,0},{32,48},{48,32},{64,80},{80,64},{96,112},{112,96},{1... | collective-permute-start | bytes 786440 | tf_op jit(solution)/shard_map/ppermute | solution.py:698
  79.2 7.1 %collective-permute-start.35 = (bf16[32,32,128]{2,1,0:T(8,128)(2,1)S(1)}, bf16[32,32,128]{2,1,0:T(8,128)(2,1)S(1)}, u32[]{:S(2)}, u32[]{:S(2)}) collective-permute-start(bf16[32,32,128]{2,1,0:T(8,128)(2,1)S(1)} %get-tuple-element.97), channel_id=1, source_target_pairs={{0,112},{16,32},{32,16},{48,64},{64,48},{80,96},{96,80},{112,0},{1... | collective-permute-start | bytes 786440 | tf_op jit(solution)/shard_map/ppermute | solution.py:698
